TPU v7x, 256 devices: a whole 4x4x8 slice. The times are simulated.
256 devices in a mesh: lon: 32 (over z, x_lo, core), lat: 8 (over y, x_hi).
Axes of the slice: x: 4 (x_hi: 2, x_lo: 2; x = x_hi * 2 + x_lo), y: 4, z: 8, core: 2. Of those that a mesh axis runs over, the one named last changes fastest.
Arguments:
- ocean_state: bfloat16 [256, 64, 4096], P(None, 'lat', 'lon'), may hold values from -6 to 6
- land_mask: int32 [64, 4096], P('lat', 'lon'), may hold values from 0 to 1, as said below
- kernel: bfloat16 [49, 256], replicated, may hold values from -2 to 2
- w_in: bfloat16 [256, 1024], replicated, may hold values from -0.375 to 0.375
- w_out: bfloat16 [1024, 256], replicated, may hold values from -0.1875 to 0.1875
- cotangent: bfloat16 [256, 64, 4096], P(None, 'lat', 'lon'), may hold values from -6 to 6
Outputs:
- stepped: bfloat16 [256, 64, 4096], P(None, 'lat', 'lon')
- grad_state: bfloat16 [256, 64, 4096], P(None, 'lat', 'lon')
- grad_kernel: float32 [49, 256], replicated
- grad_w_in: float32 [256, 1024], replicated
- grad_w_out: float32 [1024, 256], replicated
Inputs may be any that keep to these rules, and one draw needn't show every extreme that they name: `land_mask`: 1 marks an ocean cell, 0 a land cell.
All inputs are finite; a program needn't handle non-finite values.
Results may differ from a plain program's by a relative error of at most 0.0058.
Values may be sent and summed in bfloat16 or wider, within the bound.
A program may use at most 128 MiB of HBM per device.

v0:
```python
import jax
import jax.numpy as jnp
from jax import lax
from jax.sharding import PartitionSpec as P

tanh_slope = 0.7978845608028654
cubic_coef = 0.044715
norm_eps = 1e-06


def padded(block, sides, width):
    for axis, dim in sides:
        count = lax.axis_size(axis)
        forward = [(i, i + 1) for i in range(count - 1)]
        forward.append((count - 1, 0))
        backward = [(target, source) for source, target in forward]
        low = lax.ppermute(
            lax.slice_in_dim(block, block.shape[dim] - width, None, axis=dim), axis, forward
        )
        high = lax.ppermute(lax.slice_in_dim(block, 0, width, axis=dim), axis, backward)
        block = jnp.concatenate([low, block, high], axis=dim)
    return block


def gelu_pair(inputs):
    inner_arg = tanh_slope * (inputs + cubic_coef * inputs * inputs * inputs)
    tanh_val = jnp.tanh(inner_arg)
    result = 0.5 * inputs * (1.0 + tanh_val)
    derivative = 0.5 * (1.0 + tanh_val) + 0.5 * inputs * (
        1.0 - tanh_val * tanh_val
    ) * tanh_slope * (1.0 + 3.0 * cubic_coef * inputs * inputs)
    return (result, derivative)


def correlate(source, tap_weights):
    row_count = source.shape[1] - 6
    col_count = source.shape[2] - 6
    summed = jnp.zeros((source.shape[0], row_count, col_count), jnp.float32)
    for tap_row in range(7):
        for tap_col in range(7):
            weight_col = tap_weights[tap_row * 7 + tap_col][:, None, None]
            window = source[:, tap_row : tap_row + row_count, tap_col : tap_col + col_count].astype(
                jnp.float32
            )
            summed = summed + weight_col * window
    return summed


def kernel_grad(grad_field, source):
    row_count = grad_field.shape[1]
    col_count = grad_field.shape[2]
    grad_wide = grad_field.astype(jnp.float32)
    tap_sums = []
    for tap_row in range(7):
        for tap_col in range(7):
            window = source[:, tap_row : tap_row + row_count, tap_col : tap_col + col_count].astype(
                jnp.float32
            )
            tap_sums.append(jnp.sum(grad_wide * window, axis=(1, 2)))
    return jnp.stack(tap_sums)


def cell_block(conv_out, state_cells, mask_cells, cot_cells, w_in, w_out):
    chan_mean = jnp.mean(conv_out, axis=0, keepdims=True)
    centred = conv_out - chan_mean
    chan_var = jnp.mean(centred * centred, axis=0, keepdims=True)
    inv_std = lax.rsqrt(chan_var + norm_eps)
    x_hat = centred * inv_std
    normed = x_hat.astype(jnp.bfloat16)
    pre_act = lax.dot_general(
        w_in, normed, (((0,), (0,)), ((), ())), preferred_element_type=jnp.float32
    )
    act_f32, derivative = gelu_pair(pre_act)
    activated = act_f32.astype(jnp.bfloat16)
    branch = lax.dot_general(
        w_out, activated, (((0,), (0,)), ((), ())), preferred_element_type=jnp.float32
    )
    ocean_f = mask_cells.astype(jnp.float32)
    stepped = (state_cells.astype(jnp.float32) + ocean_f * branch).astype(jnp.bfloat16)
    g_branch = (ocean_f * cot_cells.astype(jnp.float32)).astype(jnp.bfloat16)
    grad_out = lax.dot_general(
        activated, g_branch, (((1,), (1,)), ((), ())), preferred_element_type=jnp.float32
    )
    g_act = jnp.dot(w_out, g_branch, preferred_element_type=jnp.float32)
    g_pre = (g_act * derivative).astype(jnp.bfloat16)
    grad_in = lax.dot_general(
        normed, g_pre, (((1,), (1,)), ((), ())), preferred_element_type=jnp.float32
    )
    g_norm = jnp.dot(w_in, g_pre, preferred_element_type=jnp.float32)
    g_mean = jnp.mean(g_norm, axis=0, keepdims=True)
    g_proj = jnp.mean(g_norm * x_hat, axis=0, keepdims=True)
    g_conv = (inv_std * (g_norm - g_mean - x_hat * g_proj)).astype(jnp.bfloat16)
    return (stepped, g_conv, grad_in, grad_out)


def extend(source):
    row_count = source.shape[1]
    with_rims = padded(source, (("lon", 2), ("lat", 1)), 3)
    band_index = lax.axis_index("lat")
    band_count = lax.axis_size("lat")
    row_ids = jnp.arange(row_count + 6)[None, :, None]
    outside = (row_ids < 3) & (band_index == 0) | (row_ids >= row_count + 3) & (
        band_index == band_count - 1
    )
    return jnp.where(outside, jnp.zeros((), source.dtype), with_rims)


def chosen(shard_rows, block_id):
    block_ids = jnp.arange(shard_rows.shape[0])
    matches = (block_ids == block_id)[:, None, None, None]
    return jnp.sum(jnp.where(matches, shard_rows.astype(jnp.float32), 0.0), axis=0)


def picker(block_ids, margin):

    def pick_rows(carried, shard_rows, first_index):
        piece_width = shard_rows.shape[3]
        left_part = chosen(shard_rows[..., piece_width - 3 :], block_ids[0])
        mid_part = chosen(shard_rows[..., margin : piece_width - margin], block_ids[1])
        right_part = chosen(shard_rows[..., :3], block_ids[2])
        return jnp.concatenate([left_part, mid_part, right_part], axis=2)

    return pick_rows


def fold_trade(top_rows, pick_rows, out_width):
    channels = top_rows.shape[1]
    initial = jnp.zeros((channels, 3, out_width), jnp.float32)
    return pick_rows(
        initial, lax.all_gather(top_rows, "lon", axis=0, tiled=True), jnp.int32(0)
    ).astype(jnp.bfloat16)


def per_device(ocean_state, land_mask, kernel, w_in, w_out, cotangent):
    channels, row_count, col_count = ocean_state.shape
    blocks = lax.axis_size("lon")
    lon_index = lax.axis_index("lon")
    crown_band = lax.axis_index("lat") == lax.axis_size("lat") - 1
    tap_weights = kernel.astype(jnp.float32)
    mirror_block = blocks - 1 - lon_index
    extended = extend(ocean_state)
    forward_ids = ((mirror_block - 1) % blocks, mirror_block, (mirror_block + 1) % blocks)
    crown_rows = fold_trade(
        ocean_state[None, :, row_count - 3 :, :], picker(forward_ids, 0), col_count + 6
    )[:, ::-1, ::-1]
    extended = jnp.concatenate(
        [
            extended[:, : row_count + 3, :],
            jnp.where(crown_band, crown_rows, extended[:, row_count + 3 :, :]),
        ],
        axis=1,
    )
    conv_out = correlate(extended, tap_weights)
    cell_count = row_count * col_count
    stepped, g_conv, grad_in, grad_out = cell_block(
        conv_out.reshape(channels, cell_count),
        ocean_state.reshape(channels, cell_count),
        land_mask.reshape(1, cell_count),
        cotangent.reshape(channels, cell_count),
        w_in,
        w_out,
    )
    stepped = stepped.reshape(channels, row_count, col_count)
    g_conv = g_conv.reshape(channels, row_count, col_count)
    grad_k = kernel_grad(g_conv, extended)
    grad_k, grad_in, grad_out = lax.psum((grad_k, grad_in, grad_out), ("lon", "lat"))
    flipped = tap_weights[::-1]
    beside_all = extend(g_conv)
    inward = correlate(beside_all, flipped)
    top_rows = jnp.pad(g_conv[:, row_count - 3 :, :], ((0, 0), (0, 6), (6, 6)))
    rim_rows = correlate(top_rows, flipped)[:, ::-1, ::-1].astype(jnp.bfloat16)
    backward_ids = ((mirror_block + 1) % blocks, mirror_block, (mirror_block - 1) % blocks)
    received = fold_trade(rim_rows[None], picker(backward_ids, 3), col_count + 6).astype(
        jnp.float32
    )
    folded = received[:, :, 3 : col_count + 3]
    folded = folded.at[:, :, :3].add(received[:, :, :3])
    folded = folded.at[:, :, col_count - 3 :].add(received[:, :, col_count + 3 :])
    grad_state = cotangent.astype(jnp.float32) + inward
    grad_state = grad_state.at[:, row_count - 3 :, :].add(jnp.where(crown_band, folded, 0.0))
    return (stepped, grad_state.astype(jnp.bfloat16), grad_k, grad_in, grad_out)


def solution(mesh):
    return jax.shard_map(
        per_device,
        mesh=mesh,
        in_specs=(P(None, "lat", "lon"), P("lat", "lon"), P(), P(), P(), P(None, "lat", "lon")),
        out_specs=(P(None, "lat", "lon"), P(None, "lat", "lon"), P(), P(), P()),
        check_vma=False,
    )
```

profile of v0, /device:TPU:1, one launch (start us, length us, event | category | flops | bytes accessed | tf_op | source)
XLA Modules:
  0.0 500.6 jit_solution(6265700278880987931)
XLA Ops:
  10.6 2.7 collective-permute-start
  26.2 1.8 collective-permute-start.2
  28.0 3.4 collective-permute-start.3
  32.0 6.4 %collective-permute-done.2 = bf16[256,3,134]{0,2,1:T(8,128)(2,1)S(1)} collective-permute-done((bf16[256,3,134]{0,2,1:T(8,128)(2,1)S(1)}, bf16[256,3,134]{0,2,1:T(8,128)(2,1)S(1)}, u32[]{:S(2)}, u32[]{:S(2)}) %collective-permute-start.2) | collective-permute-done | bytes 205856 | tf_op jit(solution)/shard_map/ppermute | solution.py:17
  38.4 5.9 %collective-permute-done.3 = bf16[256,3,134]{0,2,1:T(8,128)(2,1)S(1)} collective-permute-done((bf16[256,3,134]{0,2,1:T(8,128)(2,1)S(1)}, bf16[256,3,134]{0,2,1:T(8,128)(2,1)S(1)}, u32[]{:S(2)}, u32[]{:S(2)}) %collective-permute-start.3) | collective-permute-done | bytes 205856 | tf_op jit(solution)/shard_map/ppermute | solution.py:20
  45.7 40.1 %all-gather.5.cloned.1.call-done = bf16[8192,3,128]{2,0,1:T(8,128)(2,1)} async-done(((bf16[256,3,128]{2,0,1:T(8,128)(2,1)}), bf16[8192,3,128]{2,0,1:T(8,128)(2,1)}) %all-gather.5.cloned.1.call-update) | async-done | bytes 6291472 | tf_op jit(solution)/shard_map/all_gather | solution.py:130
  85.8 4.3 select_reduce_fusion.4
  90.4 5.2 %select_reduce_fusion.5 = (bf16[256,3,3]{2,0,1:T(8,128)(2,1)S(1)}, bf16[256,3,3]{2,0,1:T(8,128)(2,1)S(1)}) fusion(bf16[32,256,3,128]{3,1,0,2:T(8,128)(2,1)S(1)} %bitcast.220, pred[32]{0:T(512)(128)(4,1)S(1)} %get-tuple-element.193, pred[32]{0:T(512)(128)(4,1)S(1)} %get-tuple-element.192), kind=kLoop, calls=%fused_computation.54 | loop fusion | flops 437760 | bytes 304192 | tf_op jit(solution)/shard_map/reduce_sum | solution.py:111
  97.3 16.2 %fusion.137 = (f32[8,128]{1,0:T(8,128)S(1)}, f32[256,8,128]{0,2,1:T(8,128)S(1)}) fusion(bf16[256,3,134]{0,2,1:T(8,128)(2,1)S(1)} %slice_select_fusion, bf16[256,11,134]{0,2,1:T(8,128)(2,1)} %slice.1142, f32[256]{0:T(256)S(1)} %bitcast.287, f32[256]{0:T(256)S(1)} %bitcast.284, f32[256]{0:T(256)S(1)} %bitcast.281, f32[256]{0:T(256)S(1)} %bitcast.278, ...), kind=kLoop, calls=%fused_computation.365 | loop fusion | flops 55049216 | bytes 16743424 | tf_op jit(solution)/shard_map/reduce_sum | solution.py:64
  114.3 2.8 multiply_convert_fusion
  117.1 2.9 fusion.6
  124.7 7.4 %fusion.105 = (f32[256]{0:T(256)}, f32[256]{0:T(256)}, f32[256]{0:T(256)}, f32[256]{0:T(256)}, f32[256]{0:T(256)}, /*index=5*/f32[256]{0:T(256)}, f32[256]{0:T(2...) fusion(bf16[256,3,134]{0,2,1:T(8,128)(2,1)S(1)} %slice_select_fusion, bf16[256,11,134]{0,2,1:T(8,128)(2,1)} %slice.1142, ...), kind=kLoop, calls=%fused_computation.255 | loop fusion | flops 11532032 | bytes 3607552 | tf_op jit(solution)/shard_map/reduce_sum | solution.py:59
  132.2 2.1 add_add_fusion.1
  134.3 3.9 rev.8
  138.3 2.4 copy.49
  141.8 3.5 fusion.9
  145.3 2.1 fusion.106
  147.4 2.6 fusion.96
  150.0 3.3 fusion.85
  155.0 2.1 copy.64
  157.9 2.5 collective-permute-start.6
  160.5 2.6 collective-permute-start.7
  163.0 2.7 fusion.144
  165.8 5.1 %stack.199 = f32[49,256]{1,0:T(8,128)S(1)} concatenate(f32[1,256]{1,0:T(1,128)} %bitcast.386, f32[1,256]{1,0:T(1,128)} %bitcast.387, f32[1,256]{1,0:T(1,128)} %bitcast.388, f32[1,256]{1,0:T(1,128)} %bitcast.389, f32[1,256]{1,0:T(1,128)} %bitcast.390, f32[1,256]{1,0:T(1,128)} %bitcast.391, f32[1,256]{1,0:T(1,128)} %bitcast.392, f32[1,256]{1,0:T(1,128)} %bitcast.393, ...), dimensions={0} | concatenate | bytes 100352 | tf_op jit(solution)/shard_map/stack | solution.py:60
  170.9 76.7 %psum.21 = f32[49,256]{1,0:T(8,128)} all-reduce(f32[49,256]{1,0:T(8,128)S(1)} %stack.199), channel_id=1, replica_groups=mesh['lon'=32,'lat'=8] {'lon','lat'}, use_global_device_ids=true, to_apply=%region_59.60 | all-reduce | flops 12544 | bytes 100352 | tf_op jit(solution)/shard_map/psum | solution.py:166
  249.0 8.9 %add_add_fusion = f32[256,8,128]{0,2,1:T(8,128)S(1)} fusion(bf16[256,14,134]{0,2,1:T(8,128)(2,1)S(1)} %maximum_select_fusion.1, f32[256]{0:T(256)S(1)} %bitcast.289, f32[256]{0:T(256)S(1)} %bitcast.286, f32[256]{0:T(256)S(1)} %bitcast.283, f32[256]{0:T(256)S(1)} %bitcast.280, f32[256]{0:T(256)S(1)} %bitcast.277, f32[256]{0:T(256)S(1)} %bitcast.274, ...), kind=kLoop, calls=%fused_computation.267 | loop fusion | flops 38797312 | bytes 27313152 | tf_op jit(solution)/shard_map/add | solution.py:179
  258.0 13.0 %copy.66 = bf16[8192,3,134]{2,0,1:T(8,128)(2,1)} copy(bf16[8192,3,134]{0,2,1:T(8,128)(2,1)} %all-gather.7.cloned.1.call-done) | data formatting | bytes 13172736 | tf_op jit(solution)/shard_map/all_gather | solution.py:130
  271.0 8.8 %select_reduce_fusion.2 = (bf16[256,3,3]{2,0,1:T(8,128)(2,1)S(1)}, bf16[256,3,3]{2,0,1:T(8,128)(2,1)S(1)}) fusion(bf16[32,256,3,134]{3,1,0,2:T(8,128)(2,1)} %bitcast.217, pred[32]{0:T(512)(128)(4,1)S(1)} %copy-done.21, pred[32]{0:T(512)(128)(4,1)S(1)} %copy-done.23), kind=kLoop, calls=%fused_computation.51 | loop fusion | flops 437760 | bytes 304192 | tf_op jit(solution)/shard_map/reduce_sum | solution.py:111
  279.9 2.8 select_reduce_fusion.1
  284.9 204.4 %all-reduce.4.cloned.1.call-done = (f32[256,1024]{1,0:T(8,128)}, f32[1024,256]{1,0:T(8,128)}) async-done(((f32[256,1024]{1,0:T(8,128)}, f32[1024,256]{1,0:T(8,128)}), (f32[256,1024]{1,0:T(8,128)}, f32[1024,256]{1,0:T(8,128)})) %all-reduce.4.cloned.1.call-update) | async-done | bytes 2097168 | tf_op jit(solution)/shard_map/psum | solution.py:166
  489.3 2.3 copy.73
  491.6 2.3 copy.74
  (157 shorter events, 32.5 us)
Async XLA Ops:
  7.2 107.1 %copy-start = (bf16[256,1024]{1,0:T(8,128)(2,1)S(1)}, bf16[256,1024]{1,0:T(8,128)(2,1)}, u32[]{:S(2)}) copy-start(bf16[256,1024]{1,0:T(8,128)(2,1)} %param.15) | copy-start | bytes 1572868
  7.2 78.6 %all-gather.5.cloned.1.call-start = ((), (), s32[]{:S(2)}) async-start(), calls=%async_computation | async-start | bytes 6488064 | tf_op jit(solution)/shard_map/all_gather | solution.py:130
  9.2 248.8 %all-gather.7.cloned.1.call-start = ((), (), s32[]{:S(2)}) async-start(), calls=%async_computation.1 | async-start | bytes 6893568 | tf_op jit(solution)/shard_map/all_gather | solution.py:130
  10.6 15.5 %collective-permute-start = (bf16[256,8,3]{0,2,1:T(4,128)(2,1)S(1)}, bf16[256,8,3]{0,2,1:T(4,128)(2,1)S(1)}, u32[]{:S(2)}, u32[]{:S(2)}) collective-permute-start(bf16[256,8,3]{0,2,1:T(4,128)(2,1)S(1)} %get-tuple-element.135), channel_id=1, source_target_pairs={{0,8},{8,16},{16,24},{24,32},{32,40},{40,48},{48,56},{56,64},{64,7... | collective-permute-start | bytes 36872 | tf_op jit(solution)/shard_map/ppermute | solution.py:17
  13.3 12.8 %collective-permute-start.1 = (bf16[256,8,3]{0,2,1:T(4,128)(2,1)S(1)}, bf16[256,8,3]{0,2,1:T(4,128)(2,1)S(1)}, u32[]{:S(2)}, u32[]{:S(2)}) collective-permute-start(bf16[256,8,3]{0,2,1:T(4,128)(2,1)S(1)} %get-tuple-element.136), channel_id=1, source_target_pairs={{8,0},{16,8},{24,16},{32,24},{40,32},{48,40},{56,48},{64,56},{72,6... | collective-permute-start | bytes 36872 | tf_op jit(solution)/shard_map/ppermute | solution.py:20
  15.3 23.1 %copy-start.6 = (bf16[256,8,128]{0,2,1:T(8,128)(2,1)}, bf16[256,8,128]{0,2,1:T(8,128)(2,1)S(1)}, u32[]{:S(2)}) copy-start(bf16[256,8,128]{0,2,1:T(8,128)(2,1)S(1)} %copy.57) | copy-start | bytes 1572868
  15.4 74.7 %copy-start.37 = (pred[32]{0:T(512)(128)(4,1)}, pred[32]{0:T(512)(128)(4,1)S(1)}, u32[]{:S(2)}) copy-start(pred[32]{0:T(512)(128)(4,1)S(1)} %iota_compare_fusion.1) | copy-start | bytes 100
  15.4 74.7 %copy-start.20 = (pred[32]{0:T(512)(128)(4,1)}, pred[32]{0:T(512)(128)(4,1)S(1)}, u32[]{:S(2)}) copy-start(pred[32]{0:T(512)(128)(4,1)S(1)} %get-tuple-element.192) | copy-start | bytes 100
  15.4 74.7 %copy-start.22 = (pred[32]{0:T(512)(128)(4,1)}, pred[32]{0:T(512)(128)(4,1)S(1)}, u32[]{:S(2)}) copy-start(pred[32]{0:T(512)(128)(4,1)S(1)} %get-tuple-element.193) | copy-start | bytes 100
  18.0 79.2 %copy-start.12 = (f32[1,256]{1,0:T(1,128)}, f32[1,256]{1,0:T(1,128)S(1)}, u32[]{:S(2)}) copy-start(f32[1,256]{1,0:T(1,128)S(1)} %get-tuple-element.148) | copy-start | bytes 3076
  18.0 79.2 %copy-start.13 = (f32[1,256]{1,0:T(1,128)}, f32[1,256]{1,0:T(1,128)S(1)}, u32[]{:S(2)}) copy-start(f32[1,256]{1,0:T(1,128)S(1)} %get-tuple-element.149) | copy-start | bytes 3076
  18.0 79.2 %copy-start.14 = (f32[1,256]{1,0:T(1,128)}, f32[1,256]{1,0:T(1,128)S(1)}, u32[]{:S(2)}) copy-start(f32[1,256]{1,0:T(1,128)S(1)} %get-tuple-element.150) | copy-start | bytes 3076
  18.1 79.2 %copy-start.15 = (f32[1,256]{1,0:T(1,128)}, f32[1,256]{1,0:T(1,128)S(1)}, u32[]{:S(2)}) copy-start(f32[1,256]{1,0:T(1,128)S(1)} %get-tuple-element.151) | copy-start | bytes 3076
  18.1 79.2 %copy-start.16 = (f32[1,256]{1,0:T(1,128)}, f32[1,256]{1,0:T(1,128)S(1)}, u32[]{:S(2)}) copy-start(f32[1,256]{1,0:T(1,128)S(1)} %get-tuple-element.152) | copy-start | bytes 3076
  18.1 79.2 %copy-start.17 = (f32[1,256]{1,0:T(1,128)}, f32[1,256]{1,0:T(1,128)S(1)}, u32[]{:S(2)}) copy-start(f32[1,256]{1,0:T(1,128)S(1)} %get-tuple-element.153) | copy-start | bytes 3076
  18.1 79.2 %copy-start.18 = (f32[1,256]{1,0:T(1,128)}, f32[1,256]{1,0:T(1,128)S(1)}, u32[]{:S(2)}) copy-start(f32[1,256]{1,0:T(1,128)S(1)} %get-tuple-element.154) | copy-start | bytes 3076
  18.1 79.2 %copy-start.19 = (f32[1,256]{1,0:T(1,128)}, f32[1,256]{1,0:T(1,128)S(1)}, u32[]{:S(2)}) copy-start(f32[1,256]{1,0:T(1,128)S(1)} %get-tuple-element.155) | copy-start | bytes 3076
  26.1 64.0 %copy-start.39 = (pred[14]{0:T(512)(128)(4,1)}, pred[14]{0:T(512)(128)(4,1)S(1)}, u32[]{:S(2)}) copy-start(pred[14]{0:T(512)(128)(4,1)S(1)} %and_or_fusion) | copy-start | bytes 46
  26.2 12.2 %collective-permute-start.2 = (bf16[256,3,134]{0,2,1:T(8,128)(2,1)S(1)}, bf16[256,3,134]{0,2,1:T(8,128)(2,1)S(1)}, u32[]{:S(2)}, u32[]{:S(2)}) collective-permute-start(bf16[256,3,134]{0,2,1:T(8,128)(2,1)S(1)} %get-tuple-element.131), channel_id=1, source_target_pairs={{0,1},{1,2},{2,3},{3,4},{4,5},{5,6},{6,7},{7,0},{8,9},{9,10},{10,1... | collective-permute-start | bytes 617480 | tf_op jit(solution)/shard_map/ppermute | solution.py:17
  28.0 16.3 %collective-permute-start.3 = (bf16[256,3,134]{0,2,1:T(8,128)(2,1)S(1)}, bf16[256,3,134]{0,2,1:T(8,128)(2,1)S(1)}, u32[]{:S(2)}, u32[]{:S(2)}) collective-permute-start(bf16[256,3,134]{0,2,1:T(8,128)(2,1)S(1)} %get-tuple-element.132), channel_id=1, source_target_pairs={{1,0},{2,1},{3,2},{4,3},{5,4},{6,5},{7,6},{0,7},{9,8},{10,9},{11,1... | collective-permute-start | bytes 617480 | tf_op jit(solution)/shard_map/ppermute | solution.py:20
  121.4 10.8 %copy-start.28 = (f32[256]{0:T(256)S(1)}, f32[256]{0:T(256)}, u32[]{:S(2)}) copy-start(f32[256]{0:T(256)} %get-tuple-element.197) | copy-start | bytes 3076
  121.4 10.8 %copy-start.29 = (f32[256]{0:T(256)S(1)}, f32[256]{0:T(256)}, u32[]{:S(2)}) copy-start(f32[256]{0:T(256)} %get-tuple-element.198) | copy-start | bytes 3076
  121.4 10.8 %copy-start.30 = (f32[256]{0:T(256)S(1)}, f32[256]{0:T(256)}, u32[]{:S(2)}) copy-start(f32[256]{0:T(256)} %get-tuple-element.199) | copy-start | bytes 3076
  121.4 10.8 %copy-start.31 = (f32[256]{0:T(256)S(1)}, f32[256]{0:T(256)}, u32[]{:S(2)}) copy-start(f32[256]{0:T(256)} %get-tuple-element.200) | copy-start | bytes 3076
  132.1 13.3 %copy-start.3 = (bf16[256,11,134]{0,2,1:T(8,128)(2,1)S(1)}, bf16[256,11,134]{0,2,1:T(8,128)(2,1)}, u32[]{:S(2)}) copy-start(bf16[256,11,134]{0,2,1:T(8,128)(2,1)} %slice.1142) | copy-start | bytes 2264068
  138.3 351.0 %all-reduce.4.cloned.1.call-start = ((), (), s32[]{:S(2)}) async-start(), calls=%async_computation.2 | async-start | bytes 4194304 | tf_op jit(solution)/shard_map/psum | solution.py:166
  140.8 16.4 %collective-permute-start.4 = (bf16[256,8,3]{0,2,1:T(4,128)(2,1)S(1)}, bf16[256,8,3]{0,2,1:T(4,128)(2,1)S(1)}, u32[]{:S(2)}, u32[]{:S(2)}) collective-permute-start(bf16[256,8,3]{0,2,1:T(4,128)(2,1)S(1)} %get-tuple-element.133), channel_id=1, source_target_pairs={{0,8},{8,16},{16,24},{24,32},{32,40},{40,48},{48,56},{56,64},{64,7... | collective-permute-start | bytes 36872 | tf_op jit(solution)/shard_map/ppermute | solution.py:17
  141.8 15.3 %collective-permute-start.5 = (bf16[256,8,3]{0,2,1:T(4,128)(2,1)S(1)}, bf16[256,8,3]{0,2,1:T(4,128)(2,1)S(1)}, u32[]{:S(2)}, u32[]{:S(2)}) collective-permute-start(bf16[256,8,3]{0,2,1:T(4,128)(2,1)S(1)} %get-tuple-element.134), channel_id=1, source_target_pairs={{8,0},{16,8},{24,16},{32,24},{40,32},{48,40},{56,48},{64,56},{72,6... | collective-permute-start | bytes 36872 | tf_op jit(solution)/shard_map/ppermute | solution.py:20
  157.9 89.6 %collective-permute-start.6 = (bf16[256,3,134]{0,2,1:T(8,128)(2,1)}, bf16[256,3,134]{0,2,1:T(8,128)(2,1)}, u32[]{:S(2)}, u32[]{:S(2)}) collective-permute-start(bf16[256,3,134]{0,2,1:T(8,128)(2,1)} %get-tuple-element.129), channel_id=1, source_target_pairs={{0,1},{1,2},{2,3},{3,4},{4,5},{5,6},{6,7},{7,0},{8,9},{9,10},{10,1... | collective-permute-start | bytes 617480 | tf_op jit(solution)/shard_map/ppermute | solution.py:17
  160.5 87.1 %collective-permute-start.7 = (bf16[256,3,134]{0,2,1:T(8,128)(2,1)S(1)}, bf16[256,3,134]{0,2,1:T(8,128)(2,1)}, u32[]{:S(2)}, u32[]{:S(2)}) collective-permute-start(bf16[256,3,134]{0,2,1:T(8,128)(2,1)S(1)} %get-tuple-element.130), channel_id=1, source_target_pairs={{1,0},{2,1},{3,2},{4,3},{5,4},{6,5},{7,6},{0,7},{9,8},{10,9},{11,1... | collective-permute-start | bytes 617480 | tf_op jit(solution)/shard_map/ppermute | solution.py:20
  258.0 13.0 %copy-start.21 = (pred[32]{0:T(512)(128)(4,1)S(1)}, pred[32]{0:T(512)(128)(4,1)}, u32[]{:S(2)}) copy-start(pred[32]{0:T(512)(128)(4,1)} %copy-done.20) | copy-start | bytes 100
  258.0 13.0 %copy-start.23 = (pred[32]{0:T(512)(128)(4,1)S(1)}, pred[32]{0:T(512)(128)(4,1)}, u32[]{:S(2)}) copy-start(pred[32]{0:T(512)(128)(4,1)} %copy-done.22) | copy-start | bytes 100
  (19 other events, 145.2 us)
Sparse Core Ops, SparseCore 0:
  10.5 75.2 all-gather.4
  138.4 85.7 all-gather.6
  230.3 258.9 all-reduce.3
where the time goes:
time: 508 us; the launch traced here: 501 us
  waiting for transfers between devices  257 us (51%)
  other arithmetic  77.3 us (15%)
  blocking collectives  76.7 us (15%)
  local copies, waits for them, and re-layouts  44.7 us (9%)
  matrix products  15.5 us (3%)
  starting transfers between devices  14.8 us (3%)
  between operations  14.8 us (3%)
    psum x1, waiting for transfers between devices, per_device(): lax.psum((grad_k, grad_in, grad_out), ('lon', 'lat'))  204 us
    psum x1, blocking collectives, per_device(): lax.psum((grad_k, grad_in, grad_out), ('lon', 'lat'))  76.7 us
    all_gather x2, waiting for transfers between devices, fold_trade(): lax.all_gather(top_rows, 'lon', axis=0, tiled=True)  40.1 us
    reduce_sum x4, other arithmetic, chosen(): jnp.sum(jnp.where(matches, shard_rows.astype(jnp.float32), 0.0), axis=0)  21.2 us
    reduce_sum x1, other arithmetic, cell_block(): chan_mean = jnp.mean(conv_out, axis=0, keepdims=True)  16.2 us
    reduce_sum x4, other arithmetic, kernel_grad(): tap_sums.append(jnp.sum(grad_wide * window, axis=(1, 2)))  15.3 us
    all_gather x1, local copies, waits for them, and re-layouts, fold_trade(): lax.all_gather(top_rows, 'lon', axis=0, tiled=True)  13 us
    unnamed x87, local copies, waits for them, and re-layouts  12.9 us
  transfers between devices with their start and end apart: 11, of which 4 were waited for; matrix products, arithmetic and copies ran while one was open for 16% of the time, Pallas kernels for 0%

commit v1 on v0

v1 whole, which is shorter than its diff:
```python
import functools

import jax
import jax.numpy as jnp
from jax import lax
from jax.experimental import pallas as pl
from jax.experimental.pallas import tpu as pltpu
from jax.sharding import PartitionSpec as P

F32 = jnp.float32
BF16 = jnp.bfloat16
MESH = pl.DeviceIdType.MESH
TANH_SLOPE = 0.7978845608028654
CUBIC = 0.044715
EPS = 1e-06
C = 256
HID = 1024
ROWS = 8
COLS = 128
CELLS = ROWS * COLS
HALF = 2048
VMEM_LIMIT = 56 * 1024 * 1024
VSPEC = pl.BlockSpec(memory_space=pltpu.VMEM)


def al(value, multiple):
    return pl.multiple_of(value, multiple)


def lanes(rows):
    return lax.broadcasted_iota(jnp.int32, (rows, COLS), 1)


def pick(flag, yes, no):
    return flag * yes + (1 - flag) * no


class Place:
    def __init__(self, n_lon, n_lat):
        self.n_lon, self.n_lat = n_lon, n_lat
        self.lon = lax.axis_index("lon")
        self.lat = lax.axis_index("lat")
        self.crown = (self.lat == n_lat - 1).astype(jnp.int32)
        self.floor = (self.lat == 0).astype(jnp.int32)
        east = lax.rem(self.lon + 1, n_lon)
        west = lax.rem(self.lon + n_lon - 1, n_lon)
        north = pick(self.crown, self.lat, self.lat + 1)
        south = lax.rem(self.lat + n_lat - 1, n_lat)
        mirror = n_lon - 1 - self.lon
        self.west_id = {"lon": west, "lat": self.lat}
        self.east_id = {"lon": east, "lat": self.lat}
        self.north_id = {"lon": pick(self.crown, mirror, self.lon), "lat": north}
        self.south_id = {"lon": self.lon, "lat": south}
        nw = pick(self.crown, lax.rem(n_lon - self.lon, n_lon), west)
        ne = pick(self.crown, lax.rem(2 * n_lon - 2 - self.lon, n_lon), east)
        self.nw_self = (self.crown == 1) & (nw == self.lon)
        self.ne_self = (self.crown == 1) & (ne == self.lon)
        self.nw_id = {"lon": nw, "lat": north}
        self.ne_id = {"lon": ne, "lat": north}
        self.sw_id = {"lon": west, "lat": south}
        self.se_id = {"lon": east, "lat": south}
        self.core = lax.rem(self.lon, 2)
        self.xl = lax.rem(self.lon // 2, 2)
        self.zi = self.lon // 4
        self.n_xy, self.n_z = 2 * n_lat, n_lon // 4
        self.xy = self.lat * 2 + self.xl
        self.core_id = {"lon": self.lon + 1 - 2 * self.core, "lat": self.lat}

    def xy_peer(self, step):
        peer = lax.rem(self.xy + step, self.n_xy)
        return peer, {"lon": self.zi * 4 + lax.rem(peer, 2) * 2 + self.core, "lat": peer // 2}

    def z_peer(self, step):
        peer = lax.rem(self.zi + step, self.n_z)
        return peer, {"lon": peer * 4 + self.xl * 2 + self.core, "lat": self.lat}


def signal(barrier, device):
    pl.semaphore_signal(barrier, inc=1, device_id=device, device_id_type=MESH)


def greet_halo(place, barrier):
    for device in (place.west_id, place.east_id, place.north_id):
        signal(barrier, device)

    @pl.when(jnp.logical_not(place.nw_self))
    def _():
        signal(barrier, place.nw_id)

    @pl.when(jnp.logical_not(place.ne_self))
    def _():
        signal(barrier, place.ne_id)

    @pl.when(place.floor == 0)
    def _():
        for device in (place.south_id, place.sw_id, place.se_id):
            signal(barrier, device)

    return (
        5
        - place.nw_self.astype(jnp.int32)
        - place.ne_self.astype(jnp.int32)
        + 3 * (1 - place.floor)
    )


def halo_copies(place, rows_ref, t_ref, halo_ref, rt_ref, send_sem, recv_sem):
    crown = place.crown

    def remote(src, dst, index, slot, device):
        return pltpu.make_async_remote_copy(
            src_ref=src,
            dst_ref=dst,
            send_sem=send_sem.at[index],
            recv_sem=recv_sem.at[slot],
            device_id=device,
            device_id_type=MESH,
        )

    return [
        remote(t_ref, rt_ref.at[1, pl.ds(1, 2)], 0, 0, place.west_id),
        remote(t_ref, rt_ref.at[0, pl.ds(1, 2)], 1, 1, place.east_id),
        remote(rows_ref.at[pl.ds(5, 3)], halo_ref.at[crown], 2, 2 + crown, place.north_id),
        remote(rows_ref.at[pl.ds(0, 3)], halo_ref.at[1], 3, 3, place.south_id),
        remote(t_ref.at[1], rt_ref.at[1 - crown, 3 * crown], 4, 4 + 3 * crown, place.nw_id),
        remote(t_ref.at[1], rt_ref.at[crown, 3 * crown], 5, 5 + crown, place.ne_id),
        remote(t_ref.at[0], rt_ref.at[1, 3], 6, 6, place.sw_id),
        remote(t_ref.at[0], rt_ref.at[0, 3], 7, 7, place.se_id),
    ]


def halo_start(place, copies, t_ref, rt_ref, recv_sem):
    for index in (2, 0, 1):
        copies[index].start()

    @pl.when(place.floor == 0)
    def _():
        copies[3].start()
        copies[6].start()
        copies[7].start()

    for is_self, index, side, slot in ((place.nw_self, 4, 0, 7), (place.ne_self, 5, 1, 6)):

        @pl.when(is_self)
        def _(side=side, slot=slot):
            pltpu.make_async_copy(t_ref.at[1], rt_ref.at[side, 3], recv_sem.at[slot]).start()

        @pl.when(jnp.logical_not(is_self))
        def _(index=index):
            copies[index].start()


def wait_bytes(ref, sem):
    pltpu.make_async_copy(ref, ref, sem).wait()


def halo_wait(place, copies, t_ref, halo_ref, rt_ref, recv_sem):
    wait_bytes(rt_ref.at[1, pl.ds(1, 2)], recv_sem.at[0])
    wait_bytes(rt_ref.at[0, pl.ds(1, 2)], recv_sem.at[1])
    wait_bytes(halo_ref.at[1], recv_sem.at[3])
    wait_bytes(rt_ref.at[1, 3], recv_sem.at[6])
    wait_bytes(rt_ref.at[0, 3], recv_sem.at[7])

    @pl.when(place.floor == 0)
    def _():
        wait_bytes(halo_ref.at[0], recv_sem.at[2])
        wait_bytes(rt_ref.at[1, 0], recv_sem.at[4])
        wait_bytes(rt_ref.at[0, 0], recv_sem.at[5])


def halo_sent(place, copies):
    for index in (0, 1, 2):
        copies[index].wait_send()

    @pl.when(place.floor == 0)
    def _():
        for index in (3, 6, 7):
            copies[index].wait_send()

    for is_self, index in ((place.nw_self, 4), (place.ne_self, 5)):

        @pl.when(jnp.logical_not(is_self))
        def _(index=index):
            copies[index].wait_send()


def pack_group(values, group, rows_bf, edge_ref):
    lane = lanes(16)
    edge = (lane < 3) | (lane >= COLS - 3)
    packed = None
    at = pl.ds(al(group * 16, 16), 16)
    for r in range(ROWS):
        rows_bf[r, at, :] = values[r].astype(BF16)
        part = pltpu.roll(jnp.where(edge, values[r], 0.0), 8 * r + 4, 1)
        packed = part if packed is None else packed + part
    edge_ref[at, :] = packed


def pack_finish(edge_ref, t_ref):
    turned = edge_ref[...].T
    t_ref[0] = turned[:32].astype(BF16)
    t_ref[1] = turned[32:64].astype(BF16)


def unpack(place, halo_ref, rt_ref, ext_ref, rim_ref):
    crown = place.crown == 1
    source = lax.broadcasted_iota(jnp.int32, (COLS, COLS), 0)
    target = lax.broadcasted_iota(jnp.int32, (COLS, COLS), 1)
    turn = jnp.where(crown, COLS - 1 - source, source) == target
    turn = jnp.where(turn, 1.0, 0.0).astype(BF16)
    for k in range(3):
        ext_ref[k] = jnp.where(place.floor == 1, 0.0, halo_ref[0, k].astype(F32))
        row = halo_ref[1, pick(place.crown, 2 - k, k)]
        ext_ref[3 + k] = jnp.dot(row, turn, preferred_element_type=F32)
    blocks = []
    slot = lax.rem(lax.broadcasted_iota(jnp.int32, (32, C), 0), 8)
    for b in range(4):
        west, east = rt_ref[0, b].astype(F32), rt_ref[1, b].astype(F32)
        if b < 3:
            block = jnp.where(slot < 4, west, east)
        else:
            block = jnp.where((slot < 4) != crown, west, east)
        if b == 0:
            block = jnp.where(place.floor == 1, 0.0, block)
        blocks.append(block)
    rim = jnp.concatenate(blocks, axis=0).T.astype(BF16)
    last = jnp.where(crown & (source >= 96), 223 - source, source) == target
    last = jnp.where(last, 1.0, 0.0).astype(BF16)
    rim_ref[...] = jnp.dot(rim, last, preferred_element_type=F32)


def halo_kernel(n_lon, n_lat, x_ref, rows_ref, ext_ref, rim_ref, xf, rows_bf, edge, t_ref, halo, rt, send_sem, recv_sem):
    place = Place(n_lon, n_lat)
    barrier = pltpu.get_barrier_semaphore()
    count = greet_halo(place, barrier)

    def body(group, _):
        values = x_ref[pl.ds(group * 16, 16)].astype(F32).reshape(128, COLS)
        xf[pl.ds(al(group * 128, 128), 128), :] = values
        picked = [xf[pl.ds(group * 128 + r, 16, stride=8), :] for r in range(ROWS)]
        for r in range(ROWS):
            rows_ref[r, pl.ds(al(group * 16, 16), 16), :] = picked[r]
        pack_group(picked, group, rows_bf, edge)
        return 0

    lax.fori_loop(0, C // 16, body, 0)
    pack_finish(edge, t_ref)
    pl.semaphore_wait(barrier, count)
    copies = halo_copies(place, rows_bf, t_ref, halo, rt, send_sem, recv_sem)
    halo_start(place, copies, t_ref, rt, recv_sem)
    halo_wait(place, copies, t_ref, halo, rt, recv_sem)
    unpack(place, halo, rt, ext_ref, rim_ref)
    halo_sent(place, copies)


HALO_SCRATCH = [
    pltpu.VMEM((ROWS, C, COLS), BF16),
    pltpu.VMEM((C, COLS), F32),
    pltpu.VMEM((2, 32, C), BF16),
    pltpu.VMEM((2, 3, C, COLS), BF16),
    pltpu.VMEM((2, 4, 32, C), BF16),
    pltpu.SemaphoreType.DMA((8,)),
    pltpu.SemaphoreType.DMA((8,)),
]


def halo_call(x, n_lon, n_lat):
    return pl.pallas_call(
        functools.partial(halo_kernel, n_lon, n_lat),
        out_shape=(
            jax.ShapeDtypeStruct((ROWS, C, COLS), F32),
            jax.ShapeDtypeStruct((6, C, COLS), F32),
            jax.ShapeDtypeStruct((C, COLS), F32),
        ),
        in_specs=[VSPEC],
        out_specs=(VSPEC,) * 3,
        scratch_shapes=[pltpu.VMEM((C * ROWS, COLS), F32)] + HALO_SCRATCH,
        compiler_params=pltpu.CompilerParams(
            collective_id=0, has_side_effects=True, vmem_limit_bytes=VMEM_LIMIT
        ),
        name="halo_in",
    )(x)


def ext_row(rows_ref, ext_ref, r, at):
    if r < 3:
        return ext_ref[r, at, :]
    if r < 11:
        return rows_ref[r - 3, at, :]
    return ext_ref[r - 8, at, :]


def shifted(x, beside, d, lane):
    if d == 0:
        return x
    if d > 0:
        return pltpu.roll(jnp.where(lane < d, beside, x), COLS - d, 1)
    return pltpu.roll(jnp.where(lane >= COLS + d, beside, x), -d, 1)


def beside_row(rim, r):
    return pltpu.roll(rim, COLS - (8 * (r + 1) + 4) if r < 15 else 0, 1)


def conv_group(rows_ref, ext_ref, rim_ref, taps, north, group):
    at = pl.ds(al(group * 8, 8), 8)
    lane = lanes(8)
    rim = rim_ref[at, :]
    beside = [beside_row(rim, r) for r in range(14)]
    table = taps[at, :]
    table_n = table if north is None else north[at, :]
    total = [None] * ROWS
    for q in range(7):
        weight = [jnp.broadcast_to(table[:, 7 * a + q : 7 * a + q + 1], (8, COLS)) for a in range(7)]
        if north is None:
            weight_n = weight
        else:
            weight_n = [
                None if a < 4 else jnp.broadcast_to(table_n[:, 7 * a + q : 7 * a + q + 1], (8, COLS))
                for a in range(7)
            ]
        for r in range(14):
            moved = shifted(ext_row(rows_ref, ext_ref, r, at), beside[r], q - 3, lane)
            for a in range(7):
                i = r - a
                if 0 <= i < ROWS:
                    term = (weight_n if r >= 11 else weight)[a] * moved
                    total[i] = term if total[i] is None else total[i] + term
    return total


def tap_tables(taps_ref, pad_ref, fwd_ref, bwd_ref=None, north_ref=None, crown=None):
    pad_ref[...] = jnp.zeros_like(pad_ref)
    pad_ref[pl.ds(0, 49), :] = taps_ref[...].astype(F32)
    turned = pad_ref[...].T
    if fwd_ref is not None:
        fwd_ref[...] = turned
    if bwd_ref is not None:
        source = lax.broadcasted_iota(jnp.int32, (COLS, COLS), 0)
        target = lax.broadcasted_iota(jnp.int32, (COLS, COLS), 1)
        flip = jnp.where(source + target == 48, 1.0, 0.0).astype(BF16)
        flipped = jnp.dot(turned.astype(BF16), flip, preferred_element_type=F32)
        bwd_ref[...] = flipped
        north_ref[...] = jnp.where(crown, turned, flipped)


def block_kernel(
    rows_ref, ext_ref, rim_ref, mask_ref, taps_ref, w_in_ref, w_out_ref, cot_ref,
    stepped_ref, g_ref, grads_ref, gk_ref,
    pad, taps, w_in_t, w_out_t, conv, normed, gb, act, g_pre, g_norm, inv_ref, flat, gk_t,
):
    tap_tables(taps_ref, pad, taps)
    w_in_t[...] = w_in_ref[...].astype(F32).T.astype(BF16)
    w_out_t[...] = w_out_ref[...].astype(F32).T.astype(BF16)

    flat[...] = cot_ref[...].astype(F32).reshape(C * ROWS, COLS)
    for r in range(ROWS):
        ocean = mask_ref[pl.ds(r, 1), :].astype(F32)
        gb[:, r * COLS : (r + 1) * COLS] = (ocean * flat[pl.ds(r, C, stride=8), :]).astype(BF16)

    def conv_body(group, _):
        out = conv_group(rows_ref, ext_ref, rim_ref, taps, None, group)
        for i in range(ROWS):
            conv[pl.ds(al(group * 8, 8), 8), i * COLS : (i + 1) * COLS] = out[i]
        return 0

    lax.fori_loop(0, C // 8, conv_body, 0)

    for r in range(ROWS):
        at = slice(r * COLS, (r + 1) * COLS)
        value = conv[:, at]
        centred = value - jnp.sum(value, axis=0, keepdims=True) * (1.0 / C)
        var = jnp.sum(centred * centred, axis=0, keepdims=True) * (1.0 / C)
        inv = lax.rsqrt(var + EPS)
        inv_ref[pl.ds(r, 1), :] = inv
        x_hat = centred * inv
        conv[:, at] = x_hat
        normed[:, at] = x_hat.astype(BF16)

    def cells_body(n, _):
        at = pl.ds(al(n * 256, 256), 256)
        hat = normed[:, at]
        grad = gb[:, at]
        for h in range(4):
            hs = slice(h * 256, (h + 1) * 256)
            u = jnp.dot(w_in_t[hs, :], hat, preferred_element_type=F32)
            uu = u * u
            t = jnp.tanh(TANH_SLOPE * (u + CUBIC * (uu * u)))
            gate = 0.5 * (1.0 + t)
            act[hs, at] = (u * gate).astype(BF16)
            slope = gate + (0.5 * TANH_SLOPE) * u * (1.0 - t * t) * (1.0 + (3.0 * CUBIC) * uu)
            g_act = jnp.dot(w_out_ref[hs, :], grad, preferred_element_type=F32)
            g_pre[hs, at] = (g_act * slope).astype(BF16)
        g_norm[:, at] = jnp.dot(w_in_ref[...], g_pre[:, at], preferred_element_type=F32)
        branch = jnp.dot(w_out_t[...], act[:, at], preferred_element_type=F32)
        for k in range(2):
            r = 2 * n + k
            ocean = mask_ref[pl.ds(r, 1), :].astype(F32)
            flat[pl.ds(r, C, stride=8), :] = rows_ref[r] + ocean * branch[:, k * COLS : (k + 1) * COLS]
        return 0

    lax.fori_loop(0, CELLS // 256, cells_body, 0)

    def out_body(group, _):
        stepped_ref[pl.ds(group * 32, 32)] = flat[pl.ds(al(group * 256, 256), 256), :].reshape(32, ROWS, COLS).astype(BF16)
        return 0

    lax.fori_loop(0, C // 32, out_body, 0)

    nt = (((1,), (1,)), ((), ()))
    for h in range(4):
        hs = slice(h * 256, (h + 1) * 256)
        out = lax.dot_general(act[hs, :], gb[...], nt, preferred_element_type=F32).astype(BF16)
        grads_ref[h * 256 : (h + 1) * 256, :] = out[:, :COLS]
        grads_ref[1024 + h * 256 : 1024 + (h + 1) * 256, :] = out[:, COLS:]
    for h in range(4):
        hs = slice(h * 256, (h + 1) * 256)
        out = lax.dot_general(normed[...], g_pre[hs, :], nt, preferred_element_type=F32).astype(BF16)
        grads_ref[HALF + h * 512 : HALF + h * 512 + 256, :] = out[:, :COLS]
        grads_ref[HALF + h * 512 + 256 : HALF + (h + 1) * 512, :] = out[:, COLS:]

    for r in range(ROWS):
        at = slice(r * COLS, (r + 1) * COLS)
        grad, x_hat = g_norm[:, at], conv[:, at]
        mean = jnp.sum(grad, axis=0, keepdims=True) * (1.0 / C)
        proj = jnp.sum(grad * x_hat, axis=0, keepdims=True) * (1.0 / C)
        g_conv = inv_ref[pl.ds(r, 1), :] * (grad - mean - x_hat * proj)
        g_ref[r] = g_conv.astype(BF16).astype(F32)

    lane = lanes(8)

    def tap_body(group, _):
        at = pl.ds(al(group * 8, 8), 8)
        rim = rim_ref[at, :]
        beside = [beside_row(rim, r) for r in range(14)]
        grads = [g_ref[i, at, :] for i in range(ROWS)]
        out = jnp.zeros((8, COLS), F32)
        for q in range(7):
            total = [None] * 7
            for r in range(14):
                moved = shifted(ext_row(rows_ref, ext_ref, r, at), beside[r], q - 3, lane)
                for a in range(7):
                    i = r - a
                    if 0 <= i < ROWS:
                        term = grads[i] * moved
                        total[a] = term if total[a] is None else total[a] + term
            for a in range(7):
                out = jnp.where(lane == 7 * a + q, jnp.sum(total[a], axis=1, keepdims=True), out)
        gk_t[at, :] = out
        return 0

    lax.fori_loop(0, C // 8, tap_body, 0)
    turned = gk_t[...].T
    gk_ref[0] = turned[:64, :COLS].astype(BF16)
    gk_ref[1] = turned[:64, COLS:].astype(BF16)


def block_call(rows, ext, rim, mask, taps, w_in, w_out, cot):
    return pl.pallas_call(
        block_kernel,
        out_shape=(
            jax.ShapeDtypeStruct((C, ROWS, COLS), BF16),
            jax.ShapeDtypeStruct((ROWS, C, COLS), F32),
            jax.ShapeDtypeStruct((2 * HALF, COLS), BF16),
            jax.ShapeDtypeStruct((2, 64, COLS), BF16),
        ),
        in_specs=[VSPEC] * 8,
        out_specs=(VSPEC,) * 4,
        scratch_shapes=[
            pltpu.VMEM((COLS, C), F32),
            pltpu.VMEM((C, COLS), F32),
            pltpu.VMEM((HID, C), BF16),
            pltpu.VMEM((C, HID), BF16),
            pltpu.VMEM((C, CELLS), F32),
            pltpu.VMEM((C, CELLS), BF16),
            pltpu.VMEM((C, CELLS), BF16),
            pltpu.VMEM((HID, CELLS), BF16),
            pltpu.VMEM((HID, CELLS), BF16),
            pltpu.VMEM((C, CELLS), F32),
            pltpu.VMEM((ROWS, COLS), F32),
            pltpu.VMEM((C * ROWS, COLS), F32),
            pltpu.VMEM((C, COLS), F32),
        ],
        compiler_params=pltpu.CompilerParams(vmem_limit_bytes=VMEM_LIMIT),
        name="block",
    )(rows, ext, rim, mask, taps, w_in, w_out, cot)


def sum_kernel(
    n_lon, n_lat, g_ref, grads_ref, gk_ref, ext_ref, rim_ref, sums_ref, gk_out,
    rows_bf, edge, t_ref, halo, rt, send_sem, recv_sem,
    pair_in, mine, xy_in, part, z_in, done, gk_pair, gk_mine, gk_xy, gk_xy_mine, gk_z, gk_done, gk_last,
    core_sems, xy_sems, z_sems, zg_sems, xyg_sems, last_sems, gk_core, gk_xy_sems, gk_z_sems, gk_last_sems,
):
    place = Place(n_lon, n_lat)
    n_xy, n_z = place.n_xy, place.n_z
    rows_xy, rows_z = HALF // n_xy, HALF // n_xy // n_z
    barrier = pltpu.get_barrier_semaphore()
    count = greet_halo(place, barrier)
    signal(barrier, place.core_id)

    def greet_xy(step, _):
        signal(barrier, place.xy_peer(step)[1])
        return 0

    def greet_z(step, _):
        signal(barrier, place.z_peer(step)[1])
        return 0

    lax.fori_loop(1, n_xy, greet_xy, 0)
    lax.fori_loop(1, n_z, greet_z, 0)

    def body(group, _):
        at = pl.ds(al(group * 16, 16), 16)
        pack_group([g_ref[r, at, :] for r in range(ROWS)], group, rows_bf, edge)
        return 0

    lax.fori_loop(0, C // 16, body, 0)
    pack_finish(edge, t_ref)
    pl.semaphore_wait(barrier, count + n_xy + n_z - 1)

    def remote(src, dst, sems, index, device):
        return pltpu.make_async_remote_copy(
            src_ref=src, dst_ref=dst, send_sem=sems.at[0, index], recv_sem=sems.at[1, index],
            device_id=device, device_id_type=MESH,
        )

    copies = halo_copies(place, rows_bf, t_ref, halo, rt, send_sem, recv_sem)
    halo_start(place, copies, t_ref, rt, recv_sem)

    core, other = place.core, 1 - place.core
    first = remote(grads_ref.at[pl.ds(al(other * HALF, HALF), HALF)], pair_in, core_sems, 0, place.core_id)
    first_k = remote(gk_ref.at[other], gk_pair, gk_core, 0, place.core_id)
    first.start()
    first_k.start()
    first.wait()
    first_k.wait()

    def add_pair(i, _):
        at = pl.ds(al(i * 256, 256), 256)
        own = grads_ref[pl.ds(al(core * HALF + i * 256, 256), 256), :].astype(F32)
        mine[at, :] = (own + pair_in[at, :].astype(F32)).astype(BF16)
        return 0

    lax.fori_loop(0, HALF // 256, add_pair, 0)
    gk_mine[...] = (gk_ref[core].astype(F32) + gk_pair[...].astype(F32)).astype(BF16)

    def xy_copies(step):
        peer, device = place.xy_peer(step)
        return (
            remote(mine.at[pl.ds(al(peer * rows_xy, rows_xy), rows_xy)], xy_in.at[step], xy_sems, step, device),
            remote(gk_mine, gk_xy.at[step], gk_xy_sems, step, device),
        )

    def each(n, make, act):
        def run(step, _):
            for copy in make(step):
                act(copy)
            return 0

        lax.fori_loop(1, n, run, 0)

    def start(copy):
        copy.start()

    def wait(copy):
        copy.wait()

    each(n_xy, xy_copies, start)
    total = mine[pl.ds(al(place.xy * rows_xy, rows_xy), rows_xy), :].astype(F32)
    total_k = gk_mine[...].astype(F32)
    each(n_xy, xy_copies, wait)
    for step in range(1, n_xy):
        total = total + xy_in[step].astype(F32)
        total_k = total_k + gk_xy[step].astype(F32)
    part[...] = total.astype(BF16)
    gk_xy_mine[...] = total_k.astype(BF16)

    def z_copies(step):
        peer, device = place.z_peer(step)
        return (
            remote(part.at[pl.ds(al(peer * rows_z, rows_z), rows_z)], z_in.at[step], z_sems, step, device),
            remote(gk_xy_mine, gk_z.at[step], gk_z_sems, step, device),
        )

    each(n_z, z_copies, start)
    total = part[pl.ds(al(place.zi * rows_z, rows_z), rows_z), :].astype(F32)
    total_k = gk_xy_mine[...].astype(F32)
    each(n_z, z_copies, wait)
    for step in range(1, n_z):
        total = total + z_in[step].astype(F32)
        total_k = total_k + gk_z[step].astype(F32)
    done[place.xy, place.zi] = total.astype(BF16)
    gk_done[...] = total_k.astype(BF16)

    def zg_copies(step):
        _, device = place.z_peer(step)
        own = done.at[place.xy, place.zi]
        return (remote(own, own, zg_sems, step, device),)

    last_k = remote(gk_done, gk_last, gk_last_sems, 0, place.core_id)
    each(n_z, zg_copies, start)
    last_k.start()

    def zg_wait(step, _):
        sender = lax.rem(place.zi + n_z - step, n_z)
        wait_bytes(done.at[place.xy, sender], zg_sems.at[1, step])
        return 0

    lax.fori_loop(1, n_z, zg_wait, 0)

    def xyg_copies(step):
        _, device = place.xy_peer(step)
        own = done.at[place.xy]
        return (remote(own, own, xyg_sems, step, device),)

    def across(step, index):
        return remote(done.at[index], sums_ref.at[core, index], last_sems, step, place.core_id)

    each(n_xy, xyg_copies, start)
    across(0, place.xy).start()

    def xyg_wait(step, _):
        sender = lax.rem(place.xy + n_xy - step, n_xy)
        wait_bytes(done.at[sender], xyg_sems.at[1, step])
        across(step, sender).start()
        return 0

    lax.fori_loop(1, n_xy, xyg_wait, 0)
    sums_ref[core] = done[...]

    halo_wait(place, copies, t_ref, halo, rt, recv_sem)
    unpack(place, halo, rt, ext_ref, rim_ref)
    last_k.wait()
    gk_out[core] = gk_done[...]
    gk_out[other] = gk_last[...]

    def last_wait(step, _):
        sender = lax.rem(place.xy + n_xy - step, n_xy)
        wait_bytes(done.at[sender], last_sems.at[0, step])
        wait_bytes(sums_ref.at[other, sender], last_sems.at[1, step])
        return 0

    lax.fori_loop(0, n_xy, last_wait, 0)

    def sent(copy):
        copy.wait_send()

    each(n_z, zg_copies, sent)
    each(n_xy, xyg_copies, sent)
    halo_sent(place, copies)


def sum_call(g, grads, gk, n_lon, n_lat):
    n_xy, n_z = 2 * n_lat, n_lon // 4
    rows_xy, rows_z = HALF // n_xy, HALF // n_xy // n_z
    small = pltpu.VMEM((64, COLS), BF16)
    sems = lambda n: pltpu.SemaphoreType.DMA((2, n))
    return pl.pallas_call(
        functools.partial(sum_kernel, n_lon, n_lat),
        out_shape=(
            jax.ShapeDtypeStruct((6, C, COLS), F32),
            jax.ShapeDtypeStruct((C, COLS), F32),
            jax.ShapeDtypeStruct((2, n_xy, n_z, rows_z, COLS), BF16),
            jax.ShapeDtypeStruct((2, 64, COLS), BF16),
        ),
        in_specs=[VSPEC] * 3,
        out_specs=(VSPEC,) * 4,
        scratch_shapes=HALO_SCRATCH
        + [
            pltpu.VMEM((HALF, COLS), BF16),
            pltpu.VMEM((HALF, COLS), BF16),
            pltpu.VMEM((n_xy, rows_xy, COLS), BF16),
            pltpu.VMEM((rows_xy, COLS), BF16),
            pltpu.VMEM((n_z, rows_z, COLS), BF16),
            pltpu.VMEM((n_xy, n_z, rows_z, COLS), BF16),
            small,
            small,
            pltpu.VMEM((n_xy, 64, COLS), BF16),
            small,
            pltpu.VMEM((n_z, 64, COLS), BF16),
            small,
            small,
            sems(1),
            sems(n_xy),
            sems(n_z),
            sems(n_z),
            sems(n_xy),
            sems(n_xy),
            sems(1),
            sems(n_xy),
            sems(n_z),
            sems(1),
        ],
        compiler_params=pltpu.CompilerParams(
            collective_id=1, has_side_effects=True, vmem_limit_bytes=VMEM_LIMIT
        ),
        name="sums",
    )(g, grads, gk)


def finish_kernel(
    g_ref, ext_ref, rim_ref, taps_ref, cot_ref, sums_ref, gk_ref,
    state_ref, gk_out, gin_ref, gout_ref, pad, taps, north, flat,
    ):
    n_lat = lax.axis_size("lat")
    crown = lax.axis_index("lat") == n_lat - 1
    tap_tables(taps_ref, pad, None, taps, north, crown)
    flat[...] = cot_ref[...].astype(F32).reshape(C * ROWS, COLS)

    def body(group, _):
        out = conv_group(g_ref, ext_ref, rim_ref, taps, north, group)
        for i in range(ROWS):
            at = pl.ds(group * 64 + i, 8, stride=8)
            flat[at, :] = flat[at, :] + out[i]
        return 0

    lax.fori_loop(0, C // 8, body, 0)

    def out_body(group, _):
        state_ref[pl.ds(group * 32, 32)] = flat[pl.ds(al(group * 256, 256), 256), :].reshape(32, ROWS, COLS).astype(BF16)
        return 0

    lax.fori_loop(0, C // 32, out_body, 0)
    for b in range(2):
        gout_ref[:, b * COLS : (b + 1) * COLS] = sums_ref[b * 1024 : (b + 1) * 1024, :].astype(F32)
        gk_out[:, b * COLS : (b + 1) * COLS] = gk_ref[b].astype(F32)[:49]
    for b in range(8):
        gin_ref[:, b * COLS : (b + 1) * COLS] = sums_ref[HALF + b * 256 : HALF + (b + 1) * 256, :].astype(F32)


def finish_call(g, ext, rim, taps, cot, sums, gk):
    return pl.pallas_call(
        finish_kernel,
        out_shape=(
            jax.ShapeDtypeStruct((C, ROWS, COLS), BF16),
            jax.ShapeDtypeStruct((49, C), F32),
            jax.ShapeDtypeStruct((C, HID), F32),
            jax.ShapeDtypeStruct((HID, C), F32),
        ),
        in_specs=[VSPEC] * 7,
        out_specs=(VSPEC,) * 4,
        scratch_shapes=[
            pltpu.VMEM((COLS, C), F32),
            pltpu.VMEM((C, COLS), F32),
            pltpu.VMEM((C, COLS), F32),
            pltpu.VMEM((C * ROWS, COLS), F32),
        ],
        compiler_params=pltpu.CompilerParams(vmem_limit_bytes=VMEM_LIMIT),
        name="finish",
    )(g, ext, rim, taps, cot, sums, gk)


def per_device(n_lon, n_lat, ocean_state, land_mask, kernel, w_in, w_out, cotangent):
    rows, ext, rim = halo_call(ocean_state, n_lon, n_lat)
    stepped, g, grads, gk = block_call(rows, ext, rim, land_mask, kernel, w_in, w_out, cotangent)
    g_ext, g_rim, sums, gk = sum_call(g, grads, gk, n_lon, n_lat)
    state, grad_k, grad_in, grad_out = finish_call(
        g, g_ext, g_rim, kernel, cotangent, sums.reshape(2 * HALF, COLS), gk
    )
    return stepped, state, grad_k, grad_in, grad_out


def solution(mesh):
    return jax.shard_map(
        functools.partial(per_device, mesh.shape["lon"], mesh.shape["lat"]),
        mesh=mesh,
        in_specs=(P(None, "lat", "lon"), P("lat", "lon"), P(), P(), P(), P(None, "lat", "lon")),
        out_specs=(P(None, "lat", "lon"), P(None, "lat", "lon"), P(), P(), P()),
        check_vma=False,
    )
```

time: 508 us -> 123 us (0.24); the launches traced: 501 us -> 123 us
  waiting for transfers between devices: 257 us -> 0 us
  Pallas kernels: 0 us -> 122 us
  other arithmetic: 77.3 us -> 0 us
  blocking collectives: 76.7 us -> 0 us
  local copies, waits for them, and re-layouts: 44.7 us -> 0 us
  matrix products: 15.5 us -> 0 us
  starting transfers between devices: 14.8 us -> 0 us
  between operations: 14.8 us -> 0.65 us
    psum x1 -> x0, waiting for transfers between devices: 204 us -> none  [per_device(): lax.psum((grad_k, grad_in, grad_out), ('lon', 'lat'))]
    pallas_call x0 -> x4, Pallas kernels: none -> 122 us  [the longest x1 55 us: sum_call(): pl.pallas_call(functools.partial(sum_kernel, n_lon, n_lat), out_shape=(ja...]
    psum x1 -> x0, blocking collectives: 76.7 us -> none  [per_device(): lax.psum((grad_k, grad_in, grad_out), ('lon', 'lat'))]
    reduce_sum x11 -> x0, other arithmetic: 54.6 us -> none  [the longest x4 21.2 us: chosen(): jnp.sum(jnp.where(matches, shard_rows.astype(jnp.float32), 0.0), axis=0)]
    all_gather x2 -> x0, waiting for transfers between devices: 40.1 us -> none  [fold_trade(): lax.all_gather(top_rows, 'lon', axis=0, tiled=True)]
    dot_general x6 -> x0, matrix products: 15.5 us -> none  [the longest x1 3.53 us: cell_block(): lax.dot_general(w_out, activated, (((0,), (0,)), ((), ())), preferred_ele...]
    ppermute x8 -> x0, starting transfers between devices: 14.7 us -> none  [the longest x4 8.04 us: padded(): lax.ppermute(lax.slice_in_dim(block, block.shape[dim] - width, None, axis...]
    all_gather x1 -> x0, local copies, waits for them, and re-layouts: 13 us -> none  [fold_trade(): lax.all_gather(top_rows, 'lon', axis=0, tiled=True)]
  transfers between devices with their start and end apart: 11 -> 0, of which waited for: 4 -> 0; matrix products, arithmetic and copies ran while one was open for 16% -> 0% of each run, Pallas kernels for 0% -> 0%
where the time goes in v1:
time: 123 us
  Pallas kernels  122 us (99%)
    pallas_call x1, Pallas kernels, sum_call(): pl.pallas_call(functools.partial(sum_kernel, n_lon, n_lat), out_shape=(ja...  55 us
    pallas_call x1, Pallas kernels, block_call(): pl.pallas_call(block_kernel, out_shape=(jax.ShapeDtypeStruct((C, ROWS, CO...  32.9 us
    pallas_call x1, Pallas kernels, halo_call(): pl.pallas_call(functools.partial(halo_kernel, n_lon, n_lat), out_shape=(j...  20.1 us
    pallas_call x1, Pallas kernels, finish_call(): pl.pallas_call(finish_kernel, out_shape=(jax.ShapeDtypeStruct((C, ROWS, C...  14.2 us

profile of v1, /device:TPU:1, one launch (start us, length us, event | category | flops | bytes accessed | tf_op | source)
XLA Modules:
  0.0 122.8 jit_solution(3029930076911343300)
XLA Ops:
  0.6 20.1 %halo_in.1 = (f32[8,256,128]{2,1,0:T(8,128)}, f32[6,256,128]{2,1,0:T(8,128)}, f32[256,128]{1,0:T(8,128)}) custom-call(bf16[256,8,128]{2,1,0:T(8,128)(2,1)} %x_ref.1), custom_call_target="tpu_custom_call" | custom-call | tf_op jit(solution)/shard_map/halo_in/pallas_call | solution.py:268
  20.7 32.9 %block.1 = (bf16[256,8,128]{2,1,0:T(8,128)(2,1)}, f32[8,256,128]{2,1,0:T(8,128)}, bf16[4096,128]{1,0:T(8,128)(2,1)}, bf16[2,64,128]{2,1,0:T(8,128)(2,1)}) custom-call(f32[8,256,128]{2,1,0:T(8,128)} %get-tuple-element.20.rows_ref, f32[6,256,128]{2,1,0:T(8,128)} %get-tuple-element.21.ext_ref, f32[256,128]{1,0:T(8,128)} %get-tuple-element.22.rim_ref, ...), custom_call_target="tpu_custom_call" | custom-call | tf_op jit(solution)/shard_map/block/pallas_call | solution.py:459
  53.6 55.0 %sums.1 = (f32[6,256,128]{2,1,0:T(8,128)}, f32[256,128]{1,0:T(8,128)}, bf16[2,16,8,16,128]{4,3,2,1,0:T(8,128)(2,1)}, bf16[2,64,128]{2,1,0:T(8,128)(2,1)}) custom-call(f32[8,256,128]{2,1,0:T(8,128)} %get-tuple-element.24.g_ref, bf16[4096,128]{1,0:T(8,128)(2,1)} %get-tuple-element.25.grads_ref, bf16[2,64,128]{2,1,0:T(8,128)(2,1)} %get-tuple-element.26.gk_ref), custom_call_target="tpu_custom_call" | custom-call | tf_op jit(solution)/shard_map/sums/pallas_call | solution.py:659
  108.6 14.2 %finish.1 = (bf16[256,8,128]{2,1,0:T(8,128)(2,1)}, f32[49,256]{1,0:T(8,128)}, f32[256,1024]{1,0:T(8,128)}, f32[1024,256]{1,0:T(8,128)}) custom-call(f32[8,256,128]{2,1,0:T(8,128)} %get-tuple-element.24.g_ref, f32[6,256,128]{2,1,0:T(8,128)} %get-tuple-element.27.ext_ref, f32[256,128]{1,0:T(8,128)} %get-tuple-element.28.rim_ref, bf16[49,256]{1,0:T(8,128)(2,1)} %taps_ref.3, ...), custom_call_target="tpu_custom_call" | custom-call | tf_op jit(solution)/shard_map/finish/pallas_call | solution.py:733

commit v2 on v1

v2 whole, which is shorter than its diff:
```python
import functools

import jax
import jax.numpy as jnp
from jax import lax
from jax.experimental import pallas as pl
from jax.experimental.pallas import tpu as pltpu
from jax.sharding import PartitionSpec as P

F32 = jnp.float32
BF16 = jnp.bfloat16
MESH = pl.DeviceIdType.MESH
TANH_SLOPE = 0.7978845608028654
CUBIC = 0.044715
EPS = 1e-06
C = 256
HID = 1024
ROWS = 8
COLS = 128
CELLS = ROWS * COLS
HALF = 2048
VMEM_LIMIT = 56 * 1024 * 1024
VSPEC = pl.BlockSpec(memory_space=pltpu.VMEM)


def al(value, multiple):
    return pl.multiple_of(value, multiple)


def pick(flag, yes, no):
    return flag * yes + (1 - flag) * no


class Place:
    def __init__(self, n_lon, n_lat):
        self.n_lon, self.n_lat = n_lon, n_lat
        self.lon = lax.axis_index("lon")
        self.lat = lax.axis_index("lat")
        self.crown = (self.lat == n_lat - 1).astype(jnp.int32)
        self.floor = (self.lat == 0).astype(jnp.int32)
        east = lax.rem(self.lon + 1, n_lon)
        west = lax.rem(self.lon + n_lon - 1, n_lon)
        north = pick(self.crown, self.lat, self.lat + 1)
        south = lax.rem(self.lat + n_lat - 1, n_lat)
        mirror = n_lon - 1 - self.lon
        self.west_id = {"lon": west, "lat": self.lat}
        self.east_id = {"lon": east, "lat": self.lat}
        self.north_id = {"lon": pick(self.crown, mirror, self.lon), "lat": north}
        self.south_id = {"lon": self.lon, "lat": south}
        nw = pick(self.crown, lax.rem(n_lon - self.lon, n_lon), west)
        ne = pick(self.crown, lax.rem(2 * n_lon - 2 - self.lon, n_lon), east)
        self.nw_self = (self.crown == 1) & (nw == self.lon)
        self.ne_self = (self.crown == 1) & (ne == self.lon)
        self.nw_id = {"lon": nw, "lat": north}
        self.ne_id = {"lon": ne, "lat": north}
        self.sw_id = {"lon": west, "lat": south}
        self.se_id = {"lon": east, "lat": south}
        self.core = lax.rem(self.lon, 2)
        self.xl = lax.rem(self.lon // 2, 2)
        self.zi = self.lon // 4
        self.n_xy, self.n_z = 2 * n_lat, n_lon // 4
        self.xy = self.lat * 2 + self.xl
        self.core_id = {"lon": self.lon + 1 - 2 * self.core, "lat": self.lat}

    def xy_peer(self, step):
        peer = lax.rem(self.xy + step, self.n_xy)
        return peer, {"lon": self.zi * 4 + lax.rem(peer, 2) * 2 + self.core, "lat": peer // 2}

    def z_peer(self, step):
        peer = lax.rem(self.zi + step, self.n_z)
        return peer, {"lon": peer * 4 + self.xl * 2 + self.core, "lat": self.lat}


def signal(barrier, device):
    pl.semaphore_signal(barrier, inc=1, device_id=device, device_id_type=MESH)


def greet_halo(place, barrier):
    for device in (place.west_id, place.east_id, place.north_id):
        signal(barrier, device)

    @pl.when(jnp.logical_not(place.nw_self))
    def _():
        signal(barrier, place.nw_id)

    @pl.when(jnp.logical_not(place.ne_self))
    def _():
        signal(barrier, place.ne_id)

    @pl.when(place.floor == 0)
    def _():
        for device in (place.south_id, place.sw_id, place.se_id):
            signal(barrier, device)

    return (
        5
        - place.nw_self.astype(jnp.int32)
        - place.ne_self.astype(jnp.int32)
        + 3 * (1 - place.floor)
    )


def halo_copies(place, rows_ref, edges, halo_ref, rt_ref, send_sem, recv_sem):
    crown = place.crown

    def remote(src, dst, index, slot, device):
        return pltpu.make_async_remote_copy(
            src_ref=src,
            dst_ref=dst,
            send_sem=send_sem.at[index],
            recv_sem=recv_sem.at[slot],
            device_id=device,
            device_id_type=MESH,
        )

    return [
        remote(edges.at[0], rt_ref.at[1, pl.ds(1, 2)], 0, 0, place.west_id),
        remote(edges.at[1], rt_ref.at[0, pl.ds(1, 2)], 1, 1, place.east_id),
        remote(rows_ref.at[pl.ds(5, 3)], halo_ref.at[crown], 2, 2 + crown, place.north_id),
        remote(rows_ref.at[pl.ds(0, 3)], halo_ref.at[1], 3, 3, place.south_id),
        remote(edges.at[0, 1], rt_ref.at[1 - crown, 3 * crown], 4, 4 + 3 * crown, place.nw_id),
        remote(edges.at[1, 1], rt_ref.at[crown, 3 * crown], 5, 5 + crown, place.ne_id),
        remote(edges.at[0, 0], rt_ref.at[1, 3], 6, 6, place.sw_id),
        remote(edges.at[1, 0], rt_ref.at[0, 3], 7, 7, place.se_id),
    ]


def halo_start(place, copies, edges, rt_ref, recv_sem):
    for index in (2, 0, 1):
        copies[index].start()

    @pl.when(place.floor == 0)
    def _():
        copies[3].start()
        copies[6].start()
        copies[7].start()

    for is_self, index, side, slot in ((place.nw_self, 4, 0, 7), (place.ne_self, 5, 1, 6)):

        @pl.when(is_self)
        def _(side=side, slot=slot):
            pltpu.make_async_copy(edges.at[side, 1], rt_ref.at[side, 3], recv_sem.at[slot]).start()

        @pl.when(jnp.logical_not(is_self))
        def _(index=index):
            copies[index].start()


def wait_bytes(ref, sem):
    pltpu.make_async_copy(ref, ref, sem).wait()


def halo_wait(place, halo_ref, rt_ref, recv_sem):
    wait_bytes(rt_ref.at[1, pl.ds(1, 2)], recv_sem.at[0])
    wait_bytes(rt_ref.at[0, pl.ds(1, 2)], recv_sem.at[1])
    wait_bytes(halo_ref.at[1], recv_sem.at[3])
    wait_bytes(rt_ref.at[1, 3], recv_sem.at[6])
    wait_bytes(rt_ref.at[0, 3], recv_sem.at[7])

    @pl.when(place.floor == 0)
    def _():
        wait_bytes(halo_ref.at[0], recv_sem.at[2])
        wait_bytes(rt_ref.at[1, 0], recv_sem.at[4])
        wait_bytes(rt_ref.at[0, 0], recv_sem.at[5])


def halo_sent(place, copies):
    for index in (0, 1, 2):
        copies[index].wait_send()

    @pl.when(place.floor == 0)
    def _():
        for index in (3, 6, 7):
            copies[index].wait_send()

    for is_self, index in ((place.nw_self, 4), (place.ne_self, 5)):

        @pl.when(jnp.logical_not(is_self))
        def _(index=index):
            copies[index].wait_send()


NT = (((1,), (1,)), ((), ()))


def square(n, rule):
    source = lax.broadcasted_iota(jnp.int32, (n, n), 0)
    target = lax.broadcasted_iota(jnp.int32, (n, n), 1)
    return jnp.where(rule(source, target), 1.0, 0.0).astype(BF16)


def lay_row(i, row, ident, wide, rows_t, edge_f):
    turned = lax.dot_general(ident, row, NT, preferred_element_type=F32)
    wide[0, 3 + i, 8:136, :] = turned[:, :COLS]
    wide[1, 3 + i, 8:136, :] = turned[:, COLS:]
    rows_t[i] = turned.astype(BF16)
    edge_f[0, 8 * i : 8 * i + 8, :] = turned[:8]
    edge_f[1, 8 * i : 8 * i + 8, :] = turned[120:]


def lay_edges(edge_f, edges):
    for side in range(2):
        for b in range(2):
            edges[side, b] = edge_f[side, 32 * b : 32 * b + 32, :].astype(BF16)


def unpack(place, halo_ref, rt_ref, wide):
    crown = place.crown == 1
    turn = square(COLS, lambda s, t: jnp.where(crown, COLS - 1 - s, s) == t)
    turn_small = square(32, lambda s, t: jnp.where(crown, 31 - s, s) == t)
    for k in range(3):
        south = jnp.where(place.floor == 1, 0.0, halo_ref[0, k].astype(F32))
        north = jnp.dot(turn, halo_ref[1, pick(place.crown, 2 - k, k)], preferred_element_type=F32)
        for h in range(2):
            wide[h, k, 8:136, :] = south[:, h * COLS : (h + 1) * COLS]
            wide[h, 11 + k, 8:136, :] = north[:, h * COLS : (h + 1) * COLS]
    for side in range(2):
        at = slice(136 * side, 136 * side + 8)
        for b in range(4):
            if b == 3:
                block = jnp.dot(turn_small, rt_ref[side, b], preferred_element_type=F32)
            else:
                block = rt_ref[side, b].astype(F32)
            if b == 0:
                block = jnp.where(place.floor == 1, 0.0, block)
            for s in range(4):
                r = 4 * b + s - 1
                if 0 <= r < 14:
                    for h in range(2):
                        wide[h, r, at, :] = block[8 * s : 8 * s + 8, h * COLS : (h + 1) * COLS]


LOCAL_ROWS = tuple(range(3, 11))
HALO_ROWS = (0, 1, 2, 11, 12, 13)


def conv_block(wide, weight, out_ref, h, j, rows, add):
    at = [pl.ds(al(i * COLS + j * 8, 8), 8) for i in range(ROWS)]
    total = [out_ref[h, at[i], :] if add else None for i in range(ROWS)]
    for q in range(7):
        for r in rows:
            moved = wide[h, r, pl.ds(j * 8 + (q + 5), 8), :]
            for a in range(7):
                i = r - a
                if 0 <= i < ROWS:
                    term = weight(h, a, q, r) * moved
                    total[i] = term if total[i] is None else total[i] + term
    for i in range(ROWS):
        out_ref[h, at[i], :] = total[i]


def conv_local(wide, weight, out_ref):
    def body(n, _):
        conv_block(wide, weight, out_ref, n // 14, 1 + lax.rem(n, 14), LOCAL_ROWS, False)
        return 0

    lax.fori_loop(0, 28, body, 0)


def conv_rest(wide, weight, out_ref):
    def inner(n, _):
        conv_block(wide, weight, out_ref, n // 14, 1 + lax.rem(n, 14), HALO_ROWS, True)
        return 0

    def rim(n, _):
        conv_block(wide, weight, out_ref, n // 2, 15 * lax.rem(n, 2), tuple(range(14)), False)
        return 0

    lax.fori_loop(0, 28, inner, 0)
    lax.fori_loop(0, 4, rim, 0)


def tap_sums(wide, g_wide, out_ref):
    row_id = lax.broadcasted_iota(jnp.int32, (8, COLS), 0)

    def body(n, _):
        h, q = n // 7, lax.rem(n, 7)
        total = [None] * 7
        for j in range(16):
            grads = [g_wide[h, 3 + i, 8 + 8 * j : 16 + 8 * j, :] for i in range(ROWS)]
            for r in range(14):
                moved = wide[h, r, pl.ds(q + (8 * j + 5), 8), :]
                for a in range(7):
                    i = r - a
                    if 0 <= i < ROWS:
                        term = grads[i] * moved
                        total[a] = term if total[a] is None else total[a] + term
        tile = jnp.zeros((8, COLS), F32)
        for a in range(7):
            tile = jnp.where(row_id == a, jnp.sum(total[a], axis=0, keepdims=True), tile)
        out_ref[h, q] = tile
        return 0

    lax.fori_loop(0, 14, body, 0)
    for h in range(2):
        out_ref[h, 7] = jnp.zeros((8, COLS), F32)


def whole_kernel(
    n_lon, n_lat,
    x_ref, mask_ref, taps_ref, w_in_ref, w_out_ref, cot_ref,
    stepped_ref, state_ref, gk_out, gin_ref, gout_ref,
    wide, rows_t, edge_f, edges, halo, rt, send_sem, recv_sem,
    g_wide, g_rows, g_edges, g_halo, g_rt, g_send, g_recv,
    taps, taps_n, w_in_t, w_out_t, flat, conv_t, x_hat_ref, normed, gb, act, g_pre, g_norm, inv_ref,
    grads, pair_in, mine, xy_in, part, z_in, done, sums,
    tap_acc, gk, gk_pair, gk_mine, gk_xy, gk_xy_mine, gk_z, gk_all,
    core_sems, xy_sems, z_sems, zg_sems, xyg_sems, last_sems, gk_core, gk_xy_sems, gk_z_sems, gk_last_sems,
):
    place = Place(n_lon, n_lat)
    n_xy, n_z = place.n_xy, place.n_z
    rows_xy, rows_z = HALF // n_xy, HALF // n_xy // n_z
    core, other = place.core, 1 - place.core

    barrier = pltpu.get_barrier_semaphore()
    count = greet_halo(place, barrier)
    signal(barrier, place.core_id)

    def greet_xy(step, _):
        signal(barrier, place.xy_peer(step)[1])
        return 0

    def greet_z(step, _):
        signal(barrier, place.z_peer(step)[1])
        return 0

    lax.fori_loop(1, n_xy, greet_xy, 0)
    lax.fori_loop(1, n_z, greet_z, 0)

    ident = square(COLS, lambda s, t: s == t)
    flat[...] = x_ref[...].astype(F32).reshape(C * ROWS, COLS)
    for i in range(ROWS):
        lay_row(i, flat[pl.ds(i, C, stride=8), :].astype(BF16), ident, wide, rows_t, edge_f)
    lay_edges(edge_f, edges)
    pl.semaphore_wait(barrier, count + n_xy + n_z - 1)
    copies = halo_copies(place, rows_t, edges, halo, rt, send_sem, recv_sem)
    halo_start(place, copies, edges, rt, recv_sem)

    crown = place.crown == 1
    table = taps_ref[...].astype(F32)
    for t in range(49):
        for h in range(2):
            taps[h, t] = jnp.broadcast_to(table[t : t + 1, h * COLS : (h + 1) * COLS], (8, COLS))
    for t in range(28, 49):
        for h in range(2):
            taps_n[h, t] = jnp.where(crown, taps[h, t], taps[h, 48 - t])

    def forward(h, a, q, r):
        return taps[h, 7 * a + q]

    def backward(h, a, q, r):
        return taps_n[h, 7 * a + q] if r >= 11 else taps[h, 48 - 7 * a - q]

    conv_local(wide, forward, conv_t)
    w_in_t[...] = w_in_ref[...].astype(F32).T.astype(BF16)
    w_out_t[...] = w_out_ref[...].astype(F32).T.astype(BF16)
    flat[...] = cot_ref[...].astype(F32).reshape(C * ROWS, COLS)
    for r in range(ROWS):
        ocean = mask_ref[pl.ds(r, 1), :].astype(F32)
        gb[:, r * COLS : (r + 1) * COLS] = (ocean * flat[pl.ds(r, C, stride=8), :]).astype(BF16)

    halo_wait(place, halo, rt, recv_sem)
    unpack(place, halo, rt, wide)
    conv_rest(wide, forward, conv_t)

    for r in range(ROWS):
        at = slice(r * COLS, (r + 1) * COLS)
        value = jnp.concatenate([conv_t[0, at, :].T, conv_t[1, at, :].T], axis=0)
        centred = value - jnp.sum(value, axis=0, keepdims=True) * (1.0 / C)
        var = jnp.sum(centred * centred, axis=0, keepdims=True) * (1.0 / C)
        inv = lax.rsqrt(var + EPS)
        inv_ref[pl.ds(r, 1), :] = inv
        x_hat = centred * inv
        x_hat_ref[:, at] = x_hat
        normed[:, at] = x_hat.astype(BF16)

    def cells_body(n, _):
        at = pl.ds(al(n * 256, 256), 256)
        hat = normed[:, at]
        grad = gb[:, at]
        for h in range(4):
            hs = slice(h * 256, (h + 1) * 256)
            u = jnp.dot(w_in_t[hs, :], hat, preferred_element_type=F32)
            uu = u * u
            t = jnp.tanh(TANH_SLOPE * (u + CUBIC * (uu * u)))
            gate = 0.5 * (1.0 + t)
            act[hs, at] = (u * gate).astype(BF16)
            slope = gate + (0.5 * TANH_SLOPE) * u * (1.0 - t * t) * (1.0 + (3.0 * CUBIC) * uu)
            g_act = jnp.dot(w_out_ref[hs, :], grad, preferred_element_type=F32)
            g_pre[hs, at] = (g_act * slope).astype(BF16)
        g_norm[:, at] = jnp.dot(w_in_ref[...], g_pre[:, at], preferred_element_type=F32)
        branch = jnp.dot(w_out_t[...], act[:, at], preferred_element_type=F32)
        for k in range(2):
            r = 2 * n + k
            ocean = mask_ref[pl.ds(r, 1), :].astype(F32)
            flat[pl.ds(r, C, stride=8), :] = ocean * branch[:, k * COLS : (k + 1) * COLS]
        return 0

    lax.fori_loop(0, CELLS // 256, cells_body, 0)

    for h in range(4):
        hs = slice(h * 256, (h + 1) * 256)
        out = lax.dot_general(act[hs, :], gb[...], NT, preferred_element_type=F32).astype(BF16)
        grads[h * 256 : (h + 1) * 256, :] = out[:, :COLS]
        grads[1024 + h * 256 : 1024 + (h + 1) * 256, :] = out[:, COLS:]
    for h in range(4):
        hs = slice(h * 256, (h + 1) * 256)
        out = lax.dot_general(normed[...], g_pre[hs, :], NT, preferred_element_type=F32).astype(BF16)
        grads[HALF + h * 512 : HALF + h * 512 + 256, :] = out[:, :COLS]
        grads[HALF + h * 512 + 256 : HALF + (h + 1) * 512, :] = out[:, COLS:]

    def remote(src, dst, sems, index, device):
        return pltpu.make_async_remote_copy(
            src_ref=src, dst_ref=dst, send_sem=sems.at[0, index], recv_sem=sems.at[1, index],
            device_id=device, device_id_type=MESH,
        )

    def each(n, make, act):
        def run(step, _):
            act(make(step))
            return 0

        lax.fori_loop(1, n, run, 0)

    def start(copy):
        copy.start()

    def wait(copy):
        copy.wait()

    def sent(copy):
        copy.wait_send()

    first = remote(grads.at[pl.ds(al(other * HALF, HALF), HALF)], pair_in, core_sems, 0, place.core_id)
    first.start()

    for r in range(ROWS):
        at = slice(r * COLS, (r + 1) * COLS)
        grad, x_hat = g_norm[:, at], x_hat_ref[:, at]
        mean = jnp.sum(grad, axis=0, keepdims=True) * (1.0 / C)
        proj = jnp.sum(grad * x_hat, axis=0, keepdims=True) * (1.0 / C)
        g_conv = inv_ref[pl.ds(r, 1), :] * (grad - mean - x_hat * proj)
        lay_row(r, g_conv.astype(BF16), ident, g_wide, g_rows, edge_f)
    lay_edges(edge_f, g_edges)

    first.wait()

    def add_pair(i, _):
        at = pl.ds(al(i * 256, 256), 256)
        own = grads[pl.ds(al(core * HALF + i * 256, 256), 256), :].astype(F32)
        mine[at, :] = (own + pair_in[at, :].astype(F32)).astype(BF16)
        return 0

    lax.fori_loop(0, HALF // 256, add_pair, 0)

    def xy_copy(step):
        peer, device = place.xy_peer(step)
        return remote(mine.at[pl.ds(al(peer * rows_xy, rows_xy), rows_xy)], xy_in.at[step], xy_sems, step, device)

    each(n_xy, xy_copy, start)
    g_copies = halo_copies(place, g_rows, g_edges, g_halo, g_rt, g_send, g_recv)
    halo_start(place, g_copies, g_edges, g_rt, g_recv)

    tap_sums(wide, g_wide, tap_acc)
    for h in range(2):
        gk[h] = tap_acc[h].reshape(64, COLS).astype(BF16)
    first_k = remote(gk.at[other], gk_pair, gk_core, 0, place.core_id)
    first_k.start()

    def step_body(group, _):
        at = pl.ds(group * 32, 32)
        moved = flat[pl.ds(al(group * 256, 256), 256), :].reshape(32, ROWS, COLS)
        stepped_ref[at] = (x_ref[at].astype(F32) + moved).astype(BF16)
        return 0

    lax.fori_loop(0, C // 32, step_body, 0)
    conv_local(g_wide, backward, conv_t)

    each(n_xy, xy_copy, wait)
    total = mine[pl.ds(al(place.xy * rows_xy, rows_xy), rows_xy), :].astype(F32)
    for step in range(1, n_xy):
        total = total + xy_in[step].astype(F32)
    part[...] = total.astype(BF16)

    def z_copy(step):
        peer, device = place.z_peer(step)
        return remote(part.at[pl.ds(al(peer * rows_z, rows_z), rows_z)], z_in.at[step], z_sems, step, device)

    each(n_z, z_copy, start)

    first_k.wait()
    gk_mine[...] = (gk[core].astype(F32) + gk_pair[...].astype(F32)).astype(BF16)

    def gk_xy_copy(step):
        _, device = place.xy_peer(step)
        return remote(gk_mine, gk_xy.at[step], gk_xy_sems, step, device)

    each(n_xy, gk_xy_copy, start)

    each(n_z, z_copy, wait)
    total = part[pl.ds(al(place.zi * rows_z, rows_z), rows_z), :].astype(F32)
    for step in range(1, n_z):
        total = total + z_in[step].astype(F32)
    done[place.xy, place.zi] = total.astype(BF16)

    def zg_copy(step):
        _, device = place.z_peer(step)
        own = done.at[place.xy, place.zi]
        return remote(own, own, zg_sems, step, device)

    each(n_z, zg_copy, start)

    halo_wait(place, g_halo, g_rt, g_recv)
    unpack(place, g_halo, g_rt, g_wide)

    def zg_wait(step, _):
        sender = lax.rem(place.zi + n_z - step, n_z)
        wait_bytes(done.at[place.xy, sender], zg_sems.at[1, step])
        return 0

    lax.fori_loop(1, n_z, zg_wait, 0)

    def xyg_copy(step):
        _, device = place.xy_peer(step)
        own = done.at[place.xy]
        return remote(own, own, xyg_sems, step, device)

    def across(step, index):
        return remote(done.at[index], sums.at[index], last_sems, step, place.core_id)

    each(n_xy, xyg_copy, start)
    across(0, place.xy).start()

    each(n_xy, gk_xy_copy, wait)
    total = gk_mine[...].astype(F32)
    for step in range(1, n_xy):
        total = total + gk_xy[step].astype(F32)
    gk_xy_mine[...] = total.astype(BF16)

    def gk_z_copy(step):
        _, device = place.z_peer(step)
        return remote(gk_xy_mine, gk_z.at[step], gk_z_sems, step, device)

    each(n_z, gk_z_copy, start)

    conv_rest(g_wide, backward, conv_t)
    for r in range(ROWS):
        at = slice(r * COLS, (r + 1) * COLS)
        flat[pl.ds(r, C, stride=8), :] = jnp.concatenate([conv_t[0, at, :].T, conv_t[1, at, :].T], axis=0)

    def state_body(group, _):
        at = pl.ds(group * 32, 32)
        moved = flat[pl.ds(al(group * 256, 256), 256), :].reshape(32, ROWS, COLS)
        state_ref[at] = (cot_ref[at].astype(F32) + moved).astype(BF16)
        return 0

    lax.fori_loop(0, C // 32, state_body, 0)

    each(n_z, gk_z_copy, wait)
    total = gk_xy_mine[...].astype(F32)
    for step in range(1, n_z):
        total = total + gk_z[step].astype(F32)
    gk_all[core] = total.astype(BF16)
    last_k = remote(gk_all.at[core], gk_all.at[core], gk_last_sems, 0, place.core_id)
    last_k.start()

    def xyg_wait(step, _):
        sender = lax.rem(place.xy + n_xy - step, n_xy)
        wait_bytes(done.at[sender], xyg_sems.at[1, step])
        across(step, sender).start()
        return 0

    lax.fori_loop(1, n_xy, xyg_wait, 0)

    def last_wait(step, _):
        sender = lax.rem(place.xy + n_xy - step, n_xy)
        wait_bytes(done.at[sender], last_sems.at[0, step])
        wait_bytes(sums.at[sender], last_sems.at[1, step])
        return 0

    lax.fori_loop(0, n_xy, last_wait, 0)

    def write(out_sums, in_sums):
        out_rows = out_sums[...].reshape(HALF, COLS)
        in_rows = in_sums[...].reshape(HALF, COLS)
        for b in range(2):
            gout_ref[:, b * COLS : (b + 1) * COLS] = out_rows[b * 1024 : (b + 1) * 1024].astype(F32)
        for b in range(8):
            gin_ref[:, b * COLS : (b + 1) * COLS] = in_rows[b * 256 : (b + 1) * 256].astype(F32)

    @pl.when(core == 0)
    def _():
        write(done, sums)

    @pl.when(core == 1)
    def _():
        write(sums, done)

    wait_bytes(gk_all.at[core], gk_last_sems.at[0, 0])
    wait_bytes(gk_all.at[other], gk_last_sems.at[1, 0])
    for h in range(2):
        total = gk_all[h].astype(F32)
        for t in range(49):
            a, q = t // 7, t % 7
            gk_out[t : t + 1, h * COLS : (h + 1) * COLS] = total[8 * q + a : 8 * q + a + 1]

    each(n_z, zg_copy, sent)
    each(n_xy, xyg_copy, sent)
    halo_sent(place, copies)
    halo_sent(place, g_copies)


def halo_scratch():
    return [
        pltpu.VMEM((2, 2, 32, C), BF16),
        pltpu.VMEM((2, 3, COLS, C), BF16),
        pltpu.VMEM((2, 4, 32, C), BF16),
        pltpu.SemaphoreType.DMA((8,)),
        pltpu.SemaphoreType.DMA((8,)),
    ]


def per_device(n_lon, n_lat, ocean_state, land_mask, kernel, w_in, w_out, cotangent):
    n_xy, n_z = 2 * n_lat, n_lon // 4
    rows_xy, rows_z = HALF // n_xy, HALF // n_xy // n_z
    wide = pltpu.VMEM((2, 14, 144, COLS), F32)
    turned_rows = pltpu.VMEM((ROWS, COLS, C), BF16)
    small = pltpu.VMEM((64, COLS), BF16)
    table = pltpu.VMEM((2, 49, 8, COLS), F32)
    sems = lambda n: pltpu.SemaphoreType.DMA((2, n))
    summed = pltpu.VMEM((n_xy, n_z, rows_z, COLS), BF16)
    return pl.pallas_call(
        functools.partial(whole_kernel, n_lon, n_lat),
        out_shape=(
            jax.ShapeDtypeStruct((C, ROWS, COLS), BF16),
            jax.ShapeDtypeStruct((C, ROWS, COLS), BF16),
            jax.ShapeDtypeStruct((49, C), F32),
            jax.ShapeDtypeStruct((C, HID), F32),
            jax.ShapeDtypeStruct((HID, C), F32),
        ),
        in_specs=[VSPEC] * 6,
        out_specs=(VSPEC,) * 5,
        scratch_shapes=[wide, turned_rows, pltpu.VMEM((2, 64, C), F32)]
        + halo_scratch()
        + [wide, turned_rows]
        + halo_scratch()
        + [
            table,
            table,
            pltpu.VMEM((HID, C), BF16),
            pltpu.VMEM((C, HID), BF16),
            pltpu.VMEM((C * ROWS, COLS), F32),
            pltpu.VMEM((2, CELLS, COLS), F32),
            pltpu.VMEM((C, CELLS), F32),
            pltpu.VMEM((C, CELLS), BF16),
            pltpu.VMEM((C, CELLS), BF16),
            pltpu.VMEM((HID, CELLS), BF16),
            pltpu.VMEM((HID, CELLS), BF16),
            pltpu.VMEM((C, CELLS), F32),
            pltpu.VMEM((ROWS, COLS), F32),
            pltpu.VMEM((2 * HALF, COLS), BF16),
            pltpu.VMEM((HALF, COLS), BF16),
            pltpu.VMEM((HALF, COLS), BF16),
            pltpu.VMEM((n_xy, rows_xy, COLS), BF16),
            pltpu.VMEM((rows_xy, COLS), BF16),
            pltpu.VMEM((n_z, rows_z, COLS), BF16),
            summed,
            summed,
            pltpu.VMEM((2, 8, 8, COLS), F32),
            pltpu.VMEM((2, 64, COLS), BF16),
            small,
            small,
            pltpu.VMEM((n_xy, 64, COLS), BF16),
            small,
            pltpu.VMEM((n_z, 64, COLS), BF16),
            pltpu.VMEM((2, 64, COLS), BF16),
            sems(1),
            sems(n_xy),
            sems(n_z),
            sems(n_z),
            sems(n_xy),
            sems(n_xy),
            sems(1),
            sems(n_xy),
            sems(n_z),
            sems(1),
        ],
        compiler_params=pltpu.CompilerParams(
            collective_id=0, has_side_effects=True, vmem_limit_bytes=VMEM_LIMIT
        ),
        name="convnext",
    )(ocean_state, land_mask, kernel, w_in, w_out, cotangent)


def solution(mesh):
    return jax.shard_map(
        functools.partial(per_device, mesh.shape["lon"], mesh.shape["lat"]),
        mesh=mesh,
        in_specs=(P(None, "lat", "lon"), P("lat", "lon"), P(), P(), P(), P(None, "lat", "lon")),
        out_specs=(P(None, "lat", "lon"), P(None, "lat", "lon"), P(), P(), P()),
        check_vma=False,
    )
```

time: 123 us -> 81.1 us (0.66)
  Pallas kernels: 122 us -> 73.2 us
  local copies, waits for them, and re-layouts: 0 us -> 7.03 us
    pallas_call x4 -> x1, Pallas kernels: 122 us -> 73.2 us  [per_device(): pl.pallas_call(functools.partial(whole_kernel, n_lon, n_lat), out_shape=(...]
    unnamed x0 -> x11, local copies, waits for them, and re-layouts: none -> 7.03 us
where the time goes in v2:
time: 81.1 us; the launch traced here: 80.9 us
  Pallas kernels  73.2 us (90%)
  local copies, waits for them, and re-layouts  7.03 us (9%)
    pallas_call x1, Pallas kernels, per_device(): pl.pallas_call(functools.partial(whole_kernel, n_lon, n_lat), out_shape=(...  73.2 us
    unnamed x11, local copies, waits for them, and re-layouts  7.03 us

profile of v2, /device:TPU:1, one launch (start us, length us, event | category | flops | bytes accessed | tf_op | source)
XLA Modules:
  0.0 80.9 jit_solution(12731326998168343432)
XLA Ops:
  0.6 73.2 %convnext.1 = (bf16[256,8,128]{2,1,0:T(8,128)(2,1)}, bf16[256,8,128]{2,1,0:T(8,128)(2,1)}, f32[49,256]{1,0:T(8,128)}, f32[256,1024]{1,0:T(8,128)}, f32[1024,256]{1,0:T(8,128)}) custom-call(bf16[256,8,128]{2,1,0:T(8,128)(2,1)} %x_ref.1, s32[8,128]{1,0:T(8,128)} %mask_ref.1, bf16[49,256]{1,0:T(8,128)(2,1)} %taps_ref.1, bf16[256,1024]{1,0:T(8,128)(2,1)} %w_in_ref.1, ...), custom_call_target="tpu_custom_call" | custom-call | tf_op jit(solution)/shard_map/convnext/pallas_call | solution.py:632
  73.8 0.0 copy-start.1
  73.8 2.0 %copy.16 = bf16[256,8,128]{2,1,0:T(8,128)(2,1)} copy(bf16[256,8,128]{2,1,0:T(8,128)(2,1)} %get-tuple-element.10) | data formatting | bytes 1048576
  75.8 0.0 copy-start.2
  75.8 1.9 %copy.17 = bf16[256,8,128]{2,1,0:T(8,128)(2,1)} copy(bf16[256,8,128]{2,1,0:T(8,128)(2,1)} %get-tuple-element.11) | data formatting | bytes 1048576
  77.7 0.0 copy-done.2
  77.7 0.6 copy.18
  78.3 0.0 copy-done.1
  78.3 0.0 copy-start
  78.3 1.0 %copy.19 = f32[256,1024]{1,0:T(8,128)} copy(f32[256,1024]{1,0:T(8,128)S(1)} %copy-done.1) | data formatting | bytes 2097152
  79.3 0.6 copy-done
  79.9 1.0 %copy.20 = f32[1024,256]{1,0:T(8,128)} copy(f32[1024,256]{1,0:T(8,128)S(1)} %copy-done) | data formatting | bytes 2097152
Async XLA Ops:
  73.8 4.5 %copy-start.1 = (f32[256,1024]{1,0:T(8,128)S(1)}, f32[256,1024]{1,0:T(8,128)}, u32[]{:S(2)}) copy-start(f32[256,1024]{1,0:T(8,128)} %get-tuple-element.13) | copy-start | bytes 3145732
  75.8 1.9 %copy-start.2 = (f32[49,256]{1,0:T(8,128)S(1)}, f32[49,256]{1,0:T(8,128)}, u32[]{:S(2)}) copy-start(f32[49,256]{1,0:T(8,128)} %get-tuple-element.12) | copy-start | bytes 150532
  78.3 1.6 %copy-start = (f32[1024,256]{1,0:T(8,128)S(1)}, f32[1024,256]{1,0:T(8,128)}, u32[]{:S(2)}) copy-start(f32[1024,256]{1,0:T(8,128)} %get-tuple-element.14) | copy-start | bytes 3145732

commit v3 on v2

v3 whole, which is shorter than its diff:
```python
import functools

import jax
import jax.numpy as jnp
from jax import lax
from jax.experimental import pallas as pl
from jax.experimental.pallas import tpu as pltpu
from jax.sharding import PartitionSpec as P

F32 = jnp.float32
BF16 = jnp.bfloat16
MESH = pl.DeviceIdType.MESH
TANH_SLOPE = 0.7978845608028654
CUBIC = 0.044715
EPS = 1e-06
C = 256
HID = 1024
ROWS = 8
COLS = 128
CELLS = ROWS * COLS
HALF = 2048
VMEM_LIMIT = 56 * 1024 * 1024
VSPEC = pl.BlockSpec(memory_space=pltpu.VMEM)


def al(value, multiple):
    return pl.multiple_of(value, multiple)


def pick(flag, yes, no):
    return flag * yes + (1 - flag) * no


class Place:
    def __init__(self, n_lon, n_lat):
        self.n_lon, self.n_lat = n_lon, n_lat
        self.lon = lax.axis_index("lon")
        self.lat = lax.axis_index("lat")
        self.crown = (self.lat == n_lat - 1).astype(jnp.int32)
        self.floor = (self.lat == 0).astype(jnp.int32)
        east = lax.rem(self.lon + 1, n_lon)
        west = lax.rem(self.lon + n_lon - 1, n_lon)
        north = pick(self.crown, self.lat, self.lat + 1)
        south = lax.rem(self.lat + n_lat - 1, n_lat)
        mirror = n_lon - 1 - self.lon
        self.west_id = {"lon": west, "lat": self.lat}
        self.east_id = {"lon": east, "lat": self.lat}
        self.north_id = {"lon": pick(self.crown, mirror, self.lon), "lat": north}
        self.south_id = {"lon": self.lon, "lat": south}
        nw = pick(self.crown, lax.rem(n_lon - self.lon, n_lon), west)
        ne = pick(self.crown, lax.rem(2 * n_lon - 2 - self.lon, n_lon), east)
        self.nw_self = (self.crown == 1) & (nw == self.lon)
        self.ne_self = (self.crown == 1) & (ne == self.lon)
        self.nw_id = {"lon": nw, "lat": north}
        self.ne_id = {"lon": ne, "lat": north}
        self.sw_id = {"lon": west, "lat": south}
        self.se_id = {"lon": east, "lat": south}
        self.core = lax.rem(self.lon, 2)
        self.zi = self.lon // 4
        self.yi = self.lat // 2
        self.xi = lax.rem(self.lat, 2) * 2 + lax.rem(self.lon // 2, 2)
        self.n_y, self.n_z = n_lat // 2, n_lon // 4
        self.xz, self.n_xz = self.zi * 4 + self.xi, n_lon
        self.core_id = {"lon": self.lon + 1 - 2 * self.core, "lat": self.lat}

    def device(self, x, y, z):
        return {"lon": z * 4 + lax.rem(x, 2) * 2 + self.core, "lat": y * 2 + x // 2}

    def x_peer(self, step):
        return self.device(lax.rem(self.xi + step, 4), self.yi, self.zi)

    def z_peer(self, step):
        return self.device(self.xi, self.yi, lax.rem(self.zi + step, self.n_z))

    def y_peer(self, step):
        peer = lax.rem(self.yi + step, self.n_y)
        return peer, self.device(self.xi, peer, self.zi)

    def xz_peer(self, step):
        peer = lax.rem(self.xz + step, self.n_xz)
        return peer, self.device(lax.rem(peer, 4), self.yi, peer // 4)


def signal(barrier, device):
    pl.semaphore_signal(barrier, inc=1, device_id=device, device_id_type=MESH)


def greet_halo(place, barrier):
    for device in (place.west_id, place.east_id, place.north_id):
        signal(barrier, device)

    @pl.when(jnp.logical_not(place.nw_self))
    def _():
        signal(barrier, place.nw_id)

    @pl.when(jnp.logical_not(place.ne_self))
    def _():
        signal(barrier, place.ne_id)

    @pl.when(place.floor == 0)
    def _():
        for device in (place.south_id, place.sw_id, place.se_id):
            signal(barrier, device)

    return (
        5
        - place.nw_self.astype(jnp.int32)
        - place.ne_self.astype(jnp.int32)
        + 3 * (1 - place.floor)
    )


def halo_copies(place, rows_ref, edges, halo_ref, rt_ref, send_sem, recv_sem):
    crown = place.crown

    def remote(src, dst, index, slot, device):
        return pltpu.make_async_remote_copy(
            src_ref=src,
            dst_ref=dst,
            send_sem=send_sem.at[index],
            recv_sem=recv_sem.at[slot],
            device_id=device,
            device_id_type=MESH,
        )

    return [
        remote(edges.at[0], rt_ref.at[1, pl.ds(1, 2)], 0, 0, place.west_id),
        remote(edges.at[1], rt_ref.at[0, pl.ds(1, 2)], 1, 1, place.east_id),
        remote(edges.at[0, 1], rt_ref.at[1 - crown, 3 * crown], 2, 2 + 3 * crown, place.nw_id),
        remote(edges.at[1, 1], rt_ref.at[crown, 3 * crown], 3, 3 + crown, place.ne_id),
        remote(edges.at[0, 0], rt_ref.at[1, 3], 4, 4, place.sw_id),
        remote(edges.at[1, 0], rt_ref.at[0, 3], 5, 5, place.se_id),
    ] + [
        remote(rows_ref.at[7 - k], halo_ref.at[crown, k], 6 + k, 6 + k + 3 * crown, place.north_id)
        for k in range(3)
    ] + [
        remote(rows_ref.at[k], halo_ref.at[1, k], 9 + k, 9 + k, place.south_id) for k in range(3)
    ]


def halo_start(place, copies, edges, rt_ref, recv_sem):
    copies[0].start()
    copies[1].start()
    for is_self, index, side, slot in ((place.nw_self, 2, 0, 5), (place.ne_self, 3, 1, 4)):

        @pl.when(is_self)
        def _(side=side, slot=slot):
            pltpu.make_async_copy(edges.at[side, 1], rt_ref.at[side, 3], recv_sem.at[slot]).start()

        @pl.when(jnp.logical_not(is_self))
        def _(index=index):
            copies[index].start()

    @pl.when(place.floor == 0)
    def _():
        copies[4].start()
        copies[5].start()
        for k in range(3):
            copies[6 + k].start()
            copies[9 + k].start()

    @pl.when(place.floor == 1)
    def _():
        for k in range(3):
            copies[6 + k].start()


def wait_bytes(ref, sem):
    pltpu.make_async_copy(ref, ref, sem).wait()


def rim_wait(place, rt_ref, recv_sem):
    wait_bytes(rt_ref.at[1, pl.ds(1, 2)], recv_sem.at[0])
    wait_bytes(rt_ref.at[0, pl.ds(1, 2)], recv_sem.at[1])
    wait_bytes(rt_ref.at[1, 3], recv_sem.at[4])
    wait_bytes(rt_ref.at[0, 3], recv_sem.at[5])

    @pl.when(place.floor == 0)
    def _():
        wait_bytes(rt_ref.at[1, 0], recv_sem.at[2])
        wait_bytes(rt_ref.at[0, 0], recv_sem.at[3])


def row_wait(place, k, halo_ref, recv_sem):
    wait_bytes(halo_ref.at[1, k], recv_sem.at[9 + k])

    @pl.when(place.floor == 0)
    def _():
        wait_bytes(halo_ref.at[0, k], recv_sem.at[6 + k])


def halo_sent(place, copies):
    for index in (0, 1, 6, 7, 8):
        copies[index].wait_send()

    @pl.when(place.floor == 0)
    def _():
        for index in (4, 5, 9, 10, 11):
            copies[index].wait_send()

    for is_self, index in ((place.nw_self, 2), (place.ne_self, 3)):

        @pl.when(jnp.logical_not(is_self))
        def _(index=index):
            copies[index].wait_send()


NT = (((1,), (1,)), ((), ()))


def square(n, rule):
    source = lax.broadcasted_iota(jnp.int32, (n, n), 0)
    target = lax.broadcasted_iota(jnp.int32, (n, n), 1)
    return jnp.where(rule(source, target), 1.0, 0.0).astype(BF16)


def lay_row(i, row, ident, wide, rows_t, edge_f):
    turned = lax.dot_general(ident, row, NT, preferred_element_type=F32)
    wide[0, 3 + i, 8:136, :] = turned[:, :COLS]
    wide[1, 3 + i, 8:136, :] = turned[:, COLS:]
    rows_t[i] = turned.astype(BF16)
    edge_f[0, 8 * i : 8 * i + 8, :] = turned[:8]
    edge_f[1, 8 * i : 8 * i + 8, :] = turned[120:]


def lay_edges(edge_f, edges):
    for side in range(2):
        for b in range(2):
            edges[side, b] = edge_f[side, 32 * b : 32 * b + 32, :].astype(BF16)


def unpack_rim(place, rt_ref, wide):
    crown = place.crown == 1
    turn = square(32, lambda s, t: jnp.where(crown, 31 - s, s) == t)
    for side in range(2):
        at = slice(136 * side, 136 * side + 8)
        for b in range(4):
            if b == 3:
                block = jnp.dot(turn, rt_ref[side, b], preferred_element_type=F32)
            else:
                block = rt_ref[side, b].astype(F32)
            if b == 0:
                block = jnp.where(place.floor == 1, 0.0, block)
            for s in range(4):
                r = 4 * b + s - 1
                if 0 <= r < 14:
                    for h in range(2):
                        wide[h, r, at, :] = block[8 * s : 8 * s + 8, h * COLS : (h + 1) * COLS]


def unpack_row(place, k, halo_ref, wide):
    crown = place.crown == 1
    turn = square(COLS, lambda s, t: jnp.where(crown, COLS - 1 - s, s) == t)
    south = jnp.where(place.floor == 1, 0.0, halo_ref[0, k].astype(F32))
    north = jnp.dot(turn, halo_ref[1, k], preferred_element_type=F32)
    for h in range(2):
        wide[h, 2 - k, 8:136, :] = south[:, h * COLS : (h + 1) * COLS]
        wide[h, 11 + k, 8:136, :] = north[:, h * COLS : (h + 1) * COLS]


LOCAL_ROWS = tuple(range(3, 11))
HALO_ROWS = (0, 1, 2, 11, 12, 13)
PLACE = (6, 4, 2, 0, 1, 3, 5, 7)


def conv_block(wide, weight, out_ref, h, j, rows, add):
    at = [pl.ds(al(i * COLS + j * 8, 8), 8) for i in range(ROWS)]
    reached = [i for i in range(ROWS) if any(0 <= r - i < 7 for r in rows)]
    total = {i: out_ref[h, at[i], :] if add else None for i in reached}
    for q in range(7):
        for r in rows:
            moved = wide[h, r, pl.ds(j * 8 + (q + 5), 8), :]
            for a in range(7):
                i = r - a
                if 0 <= i < ROWS:
                    term = weight(h, a, q, r) * moved
                    total[i] = term if total[i] is None else total[i] + term
    for i in reached:
        out_ref[h, at[i], :] = total[i]


def conv_inner(wide, weight, out_ref):
    def body(n, _):
        conv_block(wide, weight, out_ref, n // 14, 1 + lax.rem(n, 14), LOCAL_ROWS, False)
        return 0

    lax.fori_loop(0, 28, body, 0)


def conv_rim(wide, weight, out_ref):
    def body(n, _):
        conv_block(wide, weight, out_ref, n // 2, 15 * lax.rem(n, 2), LOCAL_ROWS, False)
        return 0

    lax.fori_loop(0, 4, body, 0)


def conv_halo(wide, weight, out_ref, rows):
    def body(j, _):
        for h in range(2):
            conv_block(wide, weight, out_ref, h, j, rows, True)
        return 0

    lax.fori_loop(0, 16, body, 0)


def tap_sums(wide, g_wide, out_ref):
    row_id = lax.broadcasted_iota(jnp.int32, (8, COLS), 0)

    def body(n, _):
        h, q = n // 7, lax.rem(n, 7)
        total = [None] * 7
        for j in range(16):
            grads = [g_wide[h, 3 + i, 8 + 8 * j : 16 + 8 * j, :] for i in range(ROWS)]
            for r in range(14):
                moved = wide[h, r, pl.ds(q + (8 * j + 5), 8), :]
                for a in range(7):
                    i = r - a
                    if 0 <= i < ROWS:
                        term = grads[i] * moved
                        total[a] = term if total[a] is None else total[a] + term
        tile = jnp.zeros((8, COLS), F32)
        for a in range(7):
            tile = jnp.where(row_id == a, jnp.sum(total[a], axis=0, keepdims=True), tile)
        out_ref[h, q] = tile
        return 0

    lax.fori_loop(0, 14, body, 0)
    for h in range(2):
        out_ref[h, 7] = jnp.zeros((8, COLS), F32)


def whole_kernel(
    n_lon, n_lat,
    x_ref, mask_ref, taps_ref, w_in_ref, w_out_ref, cot_ref,
    stepped_ref, state_ref, sums_ref, gk_out,
    wide, rows_t, edge_f, edges, halo, rt, send_sem, recv_sem,
    g_wide, g_rows, g_edges, g_halo, g_rt, g_send, g_recv,
    taps, taps_n, w_in_t, w_out_t, flat, flat2, conv_t, x_hat_ref, normed, gb, act, g_pre, g_norm, inv_ref,
    grads, pair_in, mine, y_in, part, xz_in, done, sums,
    tap_acc, gk, gk_pair, gk_mine, gk_y, gk_x, gk_z, gk_all,
    core_sems, y_sems, xz_sems, xzg_sems, yg_sems, last_sems, gk_core, gk_y_sems, gk_x_sems, gk_z_sems, gk_last_sems,
):
    place = Place(n_lon, n_lat)
    n_y, n_z, n_xz = place.n_y, place.n_z, place.n_xz
    rows_y, rows_xz = HALF // n_y, HALF // n_y // n_xz
    core, other = place.core, 1 - place.core

    barrier = pltpu.get_barrier_semaphore()
    count = greet_halo(place, barrier)
    signal(barrier, place.core_id)

    def greet_y(step, _):
        signal(barrier, place.y_peer(step)[1])
        return 0

    def greet_xz(step, _):
        signal(barrier, place.xz_peer(step)[1])
        return 0

    lax.fori_loop(1, n_y, greet_y, 0)
    lax.fori_loop(1, n_xz, greet_xz, 0)

    ident = square(COLS, lambda s, t: s == t)
    flat[...] = x_ref[...].astype(F32).reshape(C * ROWS, COLS)
    for i in range(ROWS):
        lay_row(i, flat[pl.ds(i, C, stride=8), :].astype(BF16), ident, wide, rows_t, edge_f)
    lay_edges(edge_f, edges)
    pl.semaphore_wait(barrier, count + n_y + n_xz - 1)
    copies = halo_copies(place, rows_t, edges, halo, rt, send_sem, recv_sem)
    halo_start(place, copies, edges, rt, recv_sem)

    crown = place.crown == 1
    table = taps_ref[...].astype(F32)
    for t in range(49):
        for h in range(2):
            taps[h, t] = jnp.broadcast_to(table[t : t + 1, h * COLS : (h + 1) * COLS], (8, COLS))
    for t in range(28, 49):
        for h in range(2):
            taps_n[h, t] = jnp.where(crown, taps[h, t], taps[h, 48 - t])

    def forward(h, a, q, r):
        return taps[h, 7 * a + q]

    def backward(h, a, q, r):
        return taps_n[h, 7 * a + q] if r >= 11 else taps[h, 48 - 7 * a - q]

    conv_inner(wide, forward, conv_t)
    w_in_t[...] = w_in_ref[...].astype(F32).T.astype(BF16)
    w_out_t[...] = w_out_ref[...].astype(F32).T.astype(BF16)
    flat[...] = cot_ref[...].astype(F32).reshape(C * ROWS, COLS)
    for r in range(ROWS):
        ocean = mask_ref[pl.ds(r, 1), :].astype(F32)
        gb[:, PLACE[r] * COLS : (PLACE[r] + 1) * COLS] = (ocean * flat[pl.ds(r, C, stride=8), :]).astype(BF16)

    rim_wait(place, rt, recv_sem)
    unpack_rim(place, rt, wide)
    conv_rim(wide, forward, conv_t)

    def cells_body(n, _):
        for k in range(3):

            @pl.when(n == k + 1)
            def _(k=k):
                row_wait(place, k, halo, recv_sem)
                unpack_row(place, k, halo, wide)
                conv_halo(wide, forward, conv_t, (2 - k, 11 + k))

        at = pl.ds(al(n * 256, 256), 256)
        pair = (3 - n, 4 + n)
        for k, r in enumerate(pair):
            row_at = pl.ds(al(r * COLS, COLS), COLS)
            value = jnp.concatenate([conv_t[0, row_at, :].T, conv_t[1, row_at, :].T], axis=0)
            centred = value - jnp.sum(value, axis=0, keepdims=True) * (1.0 / C)
            var = jnp.sum(centred * centred, axis=0, keepdims=True) * (1.0 / C)
            inv = lax.rsqrt(var + EPS)
            inv_ref[pl.ds(r, 1), :] = inv
            x_hat = centred * inv
            x_hat_ref[:, pl.ds(al(n * 256 + k * COLS, COLS), COLS)] = x_hat
            normed[:, pl.ds(al(n * 256 + k * COLS, COLS), COLS)] = x_hat.astype(BF16)
        hat = normed[:, at]
        grad = gb[:, at]
        for h in range(4):
            hs = slice(h * 256, (h + 1) * 256)
            u = jnp.dot(w_in_t[hs, :], hat, preferred_element_type=F32)
            uu = u * u
            t = jnp.tanh(TANH_SLOPE * (u + CUBIC * (uu * u)))
            gate = 0.5 * (1.0 + t)
            act[hs, at] = (u * gate).astype(BF16)
            slope = gate + (0.5 * TANH_SLOPE) * u * (1.0 - t * t) * (1.0 + (3.0 * CUBIC) * uu)
            g_act = jnp.dot(w_out_ref[hs, :], grad, preferred_element_type=F32)
            g_pre[hs, at] = (g_act * slope).astype(BF16)
        g_norm[:, at] = jnp.dot(w_in_ref[...], g_pre[:, at], preferred_element_type=F32)
        branch = jnp.dot(w_out_t[...], act[:, at], preferred_element_type=F32)
        for k, r in enumerate(pair):
            ocean = mask_ref[pl.ds(r, 1), :].astype(F32)
            flat[pl.ds(r, C, stride=8), :] = ocean * branch[:, k * COLS : (k + 1) * COLS]
        return 0

    lax.fori_loop(0, ROWS // 2, cells_body, 0)

    for h in range(4):
        hs = slice(h * 256, (h + 1) * 256)
        out = lax.dot_general(act[hs, :], gb[...], NT, preferred_element_type=F32).astype(BF16)
        grads[h * 256 : (h + 1) * 256, :] = out[:, :COLS]
        grads[1024 + h * 256 : 1024 + (h + 1) * 256, :] = out[:, COLS:]
    for h in range(4):
        hs = slice(h * 256, (h + 1) * 256)
        out = lax.dot_general(normed[...], g_pre[hs, :], NT, preferred_element_type=F32).astype(BF16)
        grads[HALF + h * 512 : HALF + h * 512 + 256, :] = out[:, :COLS]
        grads[HALF + h * 512 + 256 : HALF + (h + 1) * 512, :] = out[:, COLS:]

    def remote(src, dst, sems, index, device):
        return pltpu.make_async_remote_copy(
            src_ref=src, dst_ref=dst, send_sem=sems.at[0, index], recv_sem=sems.at[1, index],
            device_id=device, device_id_type=MESH,
        )

    def each(n, make, act):
        def run(step, _):
            act(make(step))
            return 0

        lax.fori_loop(1, n, run, 0)

    def start(copy):
        copy.start()

    def wait(copy):
        copy.wait()

    def sent(copy):
        copy.wait_send()

    first = remote(grads.at[pl.ds(al(other * HALF, HALF), HALF)], pair_in, core_sems, 0, place.core_id)
    first.start()

    for r in range(ROWS):
        at = slice(PLACE[r] * COLS, (PLACE[r] + 1) * COLS)
        grad, x_hat = g_norm[:, at], x_hat_ref[:, at]
        mean = jnp.sum(grad, axis=0, keepdims=True) * (1.0 / C)
        proj = jnp.sum(grad * x_hat, axis=0, keepdims=True) * (1.0 / C)
        g_conv = inv_ref[pl.ds(r, 1), :] * (grad - mean - x_hat * proj)
        lay_row(r, g_conv.astype(BF16), ident, g_wide, g_rows, edge_f)
    lay_edges(edge_f, g_edges)
    g_copies = halo_copies(place, g_rows, g_edges, g_halo, g_rt, g_send, g_recv)
    halo_start(place, g_copies, g_edges, g_rt, g_recv)

    first.wait()

    def add_pair(i, _):
        at = pl.ds(al(i * 256, 256), 256)
        own = grads[pl.ds(al(core * HALF + i * 256, 256), 256), :].astype(F32)
        mine[at, :] = (own + pair_in[at, :].astype(F32)).astype(BF16)
        return 0

    lax.fori_loop(0, HALF // 256, add_pair, 0)

    def y_copy(step):
        peer, device = place.y_peer(step)
        return remote(mine.at[pl.ds(al(peer * rows_y, rows_y), rows_y)], y_in.at[step], y_sems, step, device)

    each(n_y, y_copy, start)

    tap_sums(wide, g_wide, tap_acc)
    for h in range(2):
        gk[h] = tap_acc[h].reshape(64, COLS)
    first_k = remote(gk.at[other], gk_pair, gk_core, 0, place.core_id)
    first_k.start()
    conv_inner(g_wide, backward, conv_t)

    each(n_y, y_copy, wait)

    def add_y(i, _):
        at = pl.ds(al(i * 128, 128), 128)
        total = mine[pl.ds(al(place.yi * rows_y + i * 128, 128), 128), :].astype(F32)
        for step in range(1, n_y):
            total = total + y_in[step, at, :].astype(F32)
        part[at, :] = total.astype(BF16)
        return 0

    lax.fori_loop(0, rows_y // 128, add_y, 0)

    def xz_copy(step):
        peer, device = place.xz_peer(step)
        return remote(part.at[pl.ds(al(peer * rows_xz, rows_xz), rows_xz)], xz_in.at[step], xz_sems, step, device)

    each(n_xz, xz_copy, start)

    first_k.wait()
    gk_mine[0] = (gk[core] + gk_pair[...]).astype(BF16)

    def gk_round(k, n, peer_of, slots, sems):
        def copy(step):
            return remote(gk_mine.at[k], slots.at[step], sems, step, peer_of(step))

        def finish():
            each(n, copy, wait)
            total = gk_mine[k].astype(F32)
            for step in range(1, n):
                total = total + slots[step].astype(F32)
            gk_mine[k + 1] = total.astype(BF16)

        each(n, copy, start)
        return finish

    gk_finish = gk_round(0, n_y, lambda step: place.y_peer(step)[1], gk_y, gk_y_sems)
    rim_wait(place, g_rt, g_recv)
    unpack_rim(place, g_rt, g_wide)
    conv_rim(g_wide, backward, conv_t)

    each(n_xz, xz_copy, wait)
    total = part[pl.ds(al(place.xz * rows_xz, rows_xz), rows_xz), :].astype(F32)
    for step in range(1, n_xz):
        total = total + xz_in[step].astype(F32)
    done[place.yi, place.xz] = total.astype(BF16)

    def xzg_copy(step):
        _, device = place.xz_peer(step)
        own = done.at[place.yi, place.xz]
        return remote(own, own, xzg_sems, step, device)

    each(n_xz, xzg_copy, start)
    gk_finish()
    gk_finish = gk_round(1, 4, place.x_peer, gk_x, gk_x_sems)

    for k in range(3):
        row_wait(place, k, g_halo, g_recv)
        unpack_row(place, k, g_halo, g_wide)

    def xzg_wait(step, _):
        sender = lax.rem(place.xz + n_xz - step, n_xz)
        wait_bytes(done.at[place.yi, sender], xzg_sems.at[1, step])
        return 0

    lax.fori_loop(1, n_xz, xzg_wait, 0)

    def yg_copy(step):
        _, device = place.y_peer(step)
        own = done.at[place.yi]
        return remote(own, own, yg_sems, step, device)

    def across(step, index):
        return remote(done.at[index], sums.at[index], last_sems, step, place.core_id)

    each(n_y, yg_copy, start)
    across(0, place.yi).start()

    gk_finish()
    gk_finish = gk_round(2, n_z, place.z_peer, gk_z, gk_z_sems)

    conv_halo(g_wide, backward, conv_t, HALO_ROWS)
    for r in range(ROWS):
        at = slice(r * COLS, (r + 1) * COLS)
        flat2[pl.ds(r, C, stride=8), :] = jnp.concatenate([conv_t[0, at, :].T, conv_t[1, at, :].T], axis=0)

    gk_finish()
    gk_all[core] = gk_mine[3]
    last_k = remote(gk_all.at[core], gk_all.at[core], gk_last_sems, 0, place.core_id)
    last_k.start()

    def out_body(group, _):
        at = pl.ds(group * 32, 32)
        rows_at = pl.ds(al(group * 256, 256), 256)
        moved = flat[rows_at, :].reshape(32, ROWS, COLS)
        stepped_ref[at] = (x_ref[at].astype(F32) + moved).astype(BF16)
        moved = flat2[rows_at, :].reshape(32, ROWS, COLS)
        state_ref[at] = (cot_ref[at].astype(F32) + moved).astype(BF16)
        return 0

    lax.fori_loop(0, C // 32, out_body, 0)

    def yg_wait(step, _):
        sender = lax.rem(place.yi + n_y - step, n_y)
        wait_bytes(done.at[sender], yg_sems.at[1, step])
        across(step, sender).start()
        return 0

    lax.fori_loop(1, n_y, yg_wait, 0)

    wait_bytes(gk_all.at[core], gk_last_sems.at[0, 0])
    wait_bytes(gk_all.at[other], gk_last_sems.at[1, 0])
    gk_out[...] = gk_all[...]
    sums_ref[core] = done[...]

    def last_wait(step, _):
        sender = lax.rem(place.yi + n_y - step, n_y)
        wait_bytes(done.at[sender], last_sems.at[0, step])
        wait_bytes(sums.at[sender], last_sems.at[1, step])
        return 0

    lax.fori_loop(0, n_y, last_wait, 0)
    sums_ref[other] = sums[...]

    each(n_xz, xzg_copy, sent)
    each(n_y, yg_copy, sent)
    halo_sent(place, copies)
    halo_sent(place, g_copies)


def finish_kernel(stepped_in, state_in, sums_ref, gk_ref, stepped_ref, state_ref, gk_out, gin_ref, gout_ref):
    stepped_ref[...] = stepped_in[...]
    state_ref[...] = state_in[...]
    for b in range(2):
        gout_ref[:, b * COLS : (b + 1) * COLS] = sums_ref[0, b * 1024 : (b + 1) * 1024, :].astype(F32)
    for b in range(8):
        gin_ref[:, b * COLS : (b + 1) * COLS] = sums_ref[1, b * 256 : (b + 1) * 256, :].astype(F32)
    for h in range(2):
        total = gk_ref[h].astype(F32)
        for t in range(49):
            a, q = t // 7, t % 7
            gk_out[t : t + 1, h * COLS : (h + 1) * COLS] = total[8 * q + a : 8 * q + a + 1]


def halo_scratch():
    return [
        pltpu.VMEM((2, 2, 32, C), BF16),
        pltpu.VMEM((2, 3, COLS, C), BF16),
        pltpu.VMEM((2, 4, 32, C), BF16),
        pltpu.SemaphoreType.DMA((12,)),
        pltpu.SemaphoreType.DMA((12,)),
    ]


def per_device(n_lon, n_lat, ocean_state, land_mask, kernel, w_in, w_out, cotangent):
    n_y, n_z, n_xz = n_lat // 2, n_lon // 4, n_lon
    rows_y, rows_xz = HALF // n_y, HALF // n_y // n_xz
    wide = pltpu.VMEM((2, 14, 144, COLS), F32)
    turned_rows = pltpu.VMEM((ROWS, COLS, C), BF16)
    table = pltpu.VMEM((2, 49, 8, COLS), F32)
    sems = lambda n: pltpu.SemaphoreType.DMA((2, n))
    summed = pltpu.VMEM((n_y, n_xz, rows_xz, COLS), BF16)
    flat = pltpu.VMEM((C * ROWS, COLS), F32)
    field = jax.ShapeDtypeStruct((C, ROWS, COLS), BF16)
    stepped, state, sums, gk = pl.pallas_call(
        functools.partial(whole_kernel, n_lon, n_lat),
        out_shape=(
            field,
            field,
            jax.ShapeDtypeStruct((2, n_y, n_xz, rows_xz, COLS), BF16),
            jax.ShapeDtypeStruct((2, 64, COLS), BF16),
        ),
        in_specs=[VSPEC] * 6,
        out_specs=(VSPEC,) * 4,
        scratch_shapes=[wide, turned_rows, pltpu.VMEM((2, 64, C), F32)]
        + halo_scratch()
        + [wide, turned_rows]
        + halo_scratch()
        + [
            table,
            table,
            pltpu.VMEM((HID, C), BF16),
            pltpu.VMEM((C, HID), BF16),
            flat,
            flat,
            pltpu.VMEM((2, CELLS, COLS), F32),
            pltpu.VMEM((C, CELLS), F32),
            pltpu.VMEM((C, CELLS), BF16),
            pltpu.VMEM((C, CELLS), BF16),
            pltpu.VMEM((HID, CELLS), BF16),
            pltpu.VMEM((HID, CELLS), BF16),
            pltpu.VMEM((C, CELLS), F32),
            pltpu.VMEM((ROWS, COLS), F32),
            pltpu.VMEM((2 * HALF, COLS), BF16),
            pltpu.VMEM((HALF, COLS), BF16),
            pltpu.VMEM((HALF, COLS), BF16),
            pltpu.VMEM((n_y, rows_y, COLS), BF16),
            pltpu.VMEM((rows_y, COLS), BF16),
            pltpu.VMEM((n_xz, rows_xz, COLS), BF16),
            summed,
            summed,
            pltpu.VMEM((2, 8, 8, COLS), F32),
            pltpu.VMEM((2, 64, COLS), F32),
            pltpu.VMEM((64, COLS), F32),
            pltpu.VMEM((4, 64, COLS), BF16),
            pltpu.VMEM((n_y, 64, COLS), BF16),
            pltpu.VMEM((4, 64, COLS), BF16),
            pltpu.VMEM((n_z, 64, COLS), BF16),
            pltpu.VMEM((2, 64, COLS), BF16),
            sems(1),
            sems(n_y),
            sems(n_xz),
            sems(n_xz),
            sems(n_y),
            sems(n_y),
            sems(1),
            sems(n_y),
            sems(4),
            sems(n_z),
            sems(1),
        ],
        compiler_params=pltpu.CompilerParams(
            collective_id=0, has_side_effects=True, vmem_limit_bytes=VMEM_LIMIT
        ),
        name="convnext",
    )(ocean_state, land_mask, kernel, w_in, w_out, cotangent)
    return pl.pallas_call(
        finish_kernel,
        out_shape=(
            field,
            field,
            jax.ShapeDtypeStruct((49, C), F32),
            jax.ShapeDtypeStruct((C, HID), F32),
            jax.ShapeDtypeStruct((HID, C), F32),
        ),
        in_specs=[VSPEC] * 4,
        out_specs=(VSPEC,) * 5,
        compiler_params=pltpu.CompilerParams(vmem_limit_bytes=VMEM_LIMIT),
        name="finish",
    )(stepped, state, sums.reshape(2, HALF, COLS), gk)


def solution(mesh):
    return jax.shard_map(
        functools.partial(per_device, mesh.shape["lon"], mesh.shape["lat"]),
        mesh=mesh,
        in_specs=(P(None, "lat", "lon"), P("lat", "lon"), P(), P(), P(), P(None, "lat", "lon")),
        out_specs=(P(None, "lat", "lon"), P(None, "lat", "lon"), P(), P(), P()),
        check_vma=False,
    )
```

time: 81.1 us -> 76 us (0.937)
  local copies, waits for them, and re-layouts: 7.03 us -> 0 us
  Pallas kernels: 73.2 us -> 75.2 us
    unnamed x11 -> x0, local copies, waits for them, and re-layouts: 7.03 us -> none
    pallas_call x0 -> x1, Pallas kernels: none -> 3.25 us  [per_device(): pl.pallas_call(finish_kernel, out_shape=(field, field, jax.ShapeDtypeStru...]
    pallas_call x1, Pallas kernels: 73.2 us -> 72 us  [per_device(): pl.pallas_call(functools.partial(whole_kernel, n_lon, n_lat), out_shape=(...]
where the time goes in v3:
time: 76 us; the launch traced here: 75.9 us
  Pallas kernels  75.2 us (99%)
    pallas_call x1, Pallas kernels, per_device(): pl.pallas_call(functools.partial(whole_kernel, n_lon, n_lat), out_shape=(...  72 us
    pallas_call x1, Pallas kernels, per_device(): pl.pallas_call(finish_kernel, out_shape=(field, field, jax.ShapeDtypeStru...  3.25 us

profile of v3, /device:TPU:1, one launch (start us, length us, event | category | flops | bytes accessed | tf_op | source)
XLA Modules:
  0.0 75.9 jit_solution(3611583275534618128)
XLA Ops:
  0.6 72.0 %convnext.1 = (bf16[256,8,128]{2,1,0:T(8,128)(2,1)}, bf16[256,8,128]{2,1,0:T(8,128)(2,1)}, bf16[2,4,32,16,128]{4,3,2,1,0:T(8,128)(2,1)}, bf16[2,64,128]{2,1,0:T(8,128)(2,1)}) custom-call(bf16[256,8,128]{2,1,0:T(8,128)(2,1)} %x_ref.1, s32[8,128]{1,0:T(8,128)} %mask_ref.1, bf16[49,256]{1,0:T(8,128)(2,1)} %taps_ref.1, bf16[256,1024]{1,0:T(8,128)(2,1)} %w_in_ref.1, ...), custom_call_target="tpu_custom_call" | custom-call | tf_op jit(solution)/shard_map/convnext/pallas_call | solution.py:675
  72.6 3.2 %finish.1 = (bf16[256,8,128]{2,1,0:T(8,128)(2,1)}, bf16[256,8,128]{2,1,0:T(8,128)(2,1)}, f32[49,256]{1,0:T(8,128)}, f32[256,1024]{1,0:T(8,128)}, f32[1024,256]{1,0:T(8,128)}) custom-call(bf16[256,8,128]{2,1,0:T(8,128)(2,1)} %get-tuple-element.9.stepped_in, bf16[256,8,128]{2,1,0:T(8,128)(2,1)} %get-tuple-element.10.state_in, bf16[2,2048,128]{2,1,0:T(8,128)(2,1)} %bitcast.1, ...), custom_call_target="tpu_custom_call" | custom-call | tf_op jit(solution)/shard_map/finish/pallas_call | solution.py:737

commit v4 on v3

--- a/solution.py
+++ b/solution.py
@@ -60,7 +60,6 @@
         self.yi = self.lat // 2
         self.xi = lax.rem(self.lat, 2) * 2 + lax.rem(self.lon // 2, 2)
         self.n_y, self.n_z = n_lat // 2, n_lon // 4
-        self.xz, self.n_xz = self.zi * 4 + self.xi, n_lon
         self.core_id = {"lon": self.lon + 1 - 2 * self.core, "lat": self.lat}
 
     def device(self, x, y, z):
@@ -76,9 +75,12 @@
         peer = lax.rem(self.yi + step, self.n_y)
         return peer, self.device(self.xi, peer, self.zi)
 
-    def xz_peer(self, step):
-        peer = lax.rem(self.xz + step, self.n_xz)
-        return peer, self.device(lax.rem(peer, 4), self.yi, peer // 4)
+    def plane(self, ahead):
+        return lax.rem(self.zi + ahead, self.n_z)
+
+    def xz_peer(self, ahead, step):
+        x = lax.rem(self.xi + step, 4)
+        return x, self.device(x, self.yi, self.plane(ahead))
 
 
 def signal(barrier, device):
@@ -155,14 +157,14 @@
     def _():
         copies[4].start()
         copies[5].start()
-        for k in range(3):
-            copies[6 + k].start()
-            copies[9 + k].start()
-
-    @pl.when(place.floor == 1)
+
+
+def row_start(place, copies, k):
+    copies[6 + k].start()
+
+    @pl.when(place.floor == 0)
     def _():
-        for k in range(3):
-            copies[6 + k].start()
+        copies[9 + k].start()
 
 
 def wait_bytes(ref, sem):
@@ -279,12 +281,12 @@
         out_ref[h, at[i], :] = total[i]
 
 
-def conv_inner(wide, weight, out_ref):
+def conv_inner(wide, weight, out_ref, h):
     def body(n, _):
-        conv_block(wide, weight, out_ref, n // 14, 1 + lax.rem(n, 14), LOCAL_ROWS, False)
-        return 0
-
-    lax.fori_loop(0, 28, body, 0)
+        conv_block(wide, weight, out_ref, h, n + 1, LOCAL_ROWS, False)
+        return 0
+
+    lax.fori_loop(0, 14, body, 0)
 
 
 def conv_rim(wide, weight, out_ref):
@@ -342,8 +344,11 @@
     core_sems, y_sems, xz_sems, xzg_sems, yg_sems, last_sems, gk_core, gk_y_sems, gk_x_sems, gk_z_sems, gk_last_sems,
 ):
     place = Place(n_lon, n_lat)
-    n_y, n_z, n_xz = place.n_y, place.n_z, place.n_xz
-    rows_y, rows_xz = HALF // n_y, HALF // n_y // n_xz
+    n_y, n_z = place.n_y, place.n_z
+    rows_p = HALF // n_y // n_z
+    rows_x = rows_p // 4
+    near = sorted(range(n_z), key=lambda ahead: min(ahead, n_z - ahead))
+    far = near[::-1]
     core, other = place.core, 1 - place.core
 
     barrier = pltpu.get_barrier_semaphore()
@@ -354,22 +359,18 @@
         signal(barrier, place.y_peer(step)[1])
         return 0
 
-    def greet_xz(step, _):
-        signal(barrier, place.xz_peer(step)[1])
+    def greet_xz(n, _):
+        signal(barrier, place.xz_peer(n // 4, lax.rem(n, 4))[1])
         return 0
 
     lax.fori_loop(1, n_y, greet_y, 0)
-    lax.fori_loop(1, n_xz, greet_xz, 0)
+    lax.fori_loop(1, 4 * n_z, greet_xz, 0)
 
     ident = square(COLS, lambda s, t: s == t)
     flat[...] = x_ref[...].astype(F32).reshape(C * ROWS, COLS)
     for i in range(ROWS):
         lay_row(i, flat[pl.ds(i, C, stride=8), :].astype(BF16), ident, wide, rows_t, edge_f)
     lay_edges(edge_f, edges)
-    pl.semaphore_wait(barrier, count + n_y + n_xz - 1)
-    copies = halo_copies(place, rows_t, edges, halo, rt, send_sem, recv_sem)
-    halo_start(place, copies, edges, rt, recv_sem)
-
     crown = place.crown == 1
     table = taps_ref[...].astype(F32)
     for t in range(49):
@@ -385,7 +386,7 @@
     def backward(h, a, q, r):
         return taps_n[h, 7 * a + q] if r >= 11 else taps[h, 48 - 7 * a - q]
 
-    conv_inner(wide, forward, conv_t)
+    conv_inner(wide, forward, conv_t, 0)
     w_in_t[...] = w_in_ref[...].astype(F32).T.astype(BF16)
     w_out_t[...] = w_out_ref[...].astype(F32).T.astype(BF16)
     flat[...] = cot_ref[...].astype(F32).reshape(C * ROWS, COLS)
@@ -393,9 +394,16 @@
         ocean = mask_ref[pl.ds(r, 1), :].astype(F32)
         gb[:, PLACE[r] * COLS : (PLACE[r] + 1) * COLS] = (ocean * flat[pl.ds(r, C, stride=8), :]).astype(BF16)
 
+    pl.semaphore_wait(barrier, count + n_y + 4 * n_z - 1)
+    copies = halo_copies(place, rows_t, edges, halo, rt, send_sem, recv_sem)
+    halo_start(place, copies, edges, rt, recv_sem)
+    row_start(place, copies, 0)
+    conv_inner(wide, forward, conv_t, 1)
+    row_start(place, copies, 1)
     rim_wait(place, rt, recv_sem)
     unpack_rim(place, rt, wide)
     conv_rim(wide, forward, conv_t)
+    row_start(place, copies, 2)
 
     def cells_body(n, _):
         for k in range(3):
@@ -430,11 +438,6 @@
             slope = gate + (0.5 * TANH_SLOPE) * u * (1.0 - t * t) * (1.0 + (3.0 * CUBIC) * uu)
             g_act = jnp.dot(w_out_ref[hs, :], grad, preferred_element_type=F32)
             g_pre[hs, at] = (g_act * slope).astype(BF16)
-        g_norm[:, at] = jnp.dot(w_in_ref[...], g_pre[:, at], preferred_element_type=F32)
-        branch = jnp.dot(w_out_t[...], act[:, at], preferred_element_type=F32)
-        for k, r in enumerate(pair):
-            ocean = mask_ref[pl.ds(r, 1), :].astype(F32)
-            flat[pl.ds(r, C, stride=8), :] = ocean * branch[:, k * COLS : (k + 1) * COLS]
         return 0
 
     lax.fori_loop(0, ROWS // 2, cells_body, 0)
@@ -475,6 +478,12 @@
     first = remote(grads.at[pl.ds(al(other * HALF, HALF), HALF)], pair_in, core_sems, 0, place.core_id)
     first.start()
 
+    def norm_body(n, _):
+        at = pl.ds(al(n * 256, 256), 256)
+        g_norm[:, at] = jnp.dot(w_in_ref[...], g_pre[:, at], preferred_element_type=F32)
+        return 0
+
+    lax.fori_loop(0, ROWS // 2, norm_body, 0)
     for r in range(ROWS):
         at = slice(PLACE[r] * COLS, (PLACE[r] + 1) * COLS)
         grad, x_hat = g_norm[:, at], x_hat_ref[:, at]
@@ -485,6 +494,8 @@
     lay_edges(edge_f, g_edges)
     g_copies = halo_copies(place, g_rows, g_edges, g_halo, g_rt, g_send, g_recv)
     halo_start(place, g_copies, g_edges, g_rt, g_recv)
+    for k in range(3):
+        row_start(place, g_copies, k)
 
     first.wait()
 
@@ -496,36 +507,51 @@
 
     lax.fori_loop(0, HALF // 256, add_pair, 0)
 
-    def y_copy(step):
+    def y_copy(ahead, step):
         peer, device = place.y_peer(step)
-        return remote(mine.at[pl.ds(al(peer * rows_y, rows_y), rows_y)], y_in.at[step], y_sems, step, device)
-
-    each(n_y, y_copy, start)
+        row = (peer * n_z + place.plane(ahead)) * rows_p
+        return remote(mine.at[pl.ds(al(row, rows_p), rows_p)], y_in.at[ahead, step], y_sems, ahead * n_y + step, device)
+
+    def plane_steps(ahead):
+        return range(1 if ahead == 0 else 0, 4)
+
+    for ahead in far:
+        for step in range(1, n_y):
+            y_copy(ahead, step).start()
 
     tap_sums(wide, g_wide, tap_acc)
     for h in range(2):
         gk[h] = tap_acc[h].reshape(64, COLS)
     first_k = remote(gk.at[other], gk_pair, gk_core, 0, place.core_id)
     first_k.start()
-    conv_inner(g_wide, backward, conv_t)
-
-    each(n_y, y_copy, wait)
-
-    def add_y(i, _):
-        at = pl.ds(al(i * 128, 128), 128)
-        total = mine[pl.ds(al(place.yi * rows_y + i * 128, 128), 128), :].astype(F32)
+
+    def xz_copy(ahead, step):
+        x, device = place.xz_peer(ahead, step)
+        src = part.at[ahead, pl.ds(al(x * rows_x, rows_x), rows_x)]
+        return remote(src, xz_in.at[ahead, step], xz_sems, ahead * 4 + step, device)
+
+    for ahead in far:
         for step in range(1, n_y):
-            total = total + y_in[step, at, :].astype(F32)
-        part[at, :] = total.astype(BF16)
-        return 0
-
-    lax.fori_loop(0, rows_y // 128, add_y, 0)
-
-    def xz_copy(step):
-        peer, device = place.xz_peer(step)
-        return remote(part.at[pl.ds(al(peer * rows_xz, rows_xz), rows_xz)], xz_in.at[step], xz_sems, step, device)
-
-    each(n_xz, xz_copy, start)
+            y_copy(ahead, step).wait()
+        own = pl.ds(al((place.yi * n_z + place.plane(ahead)) * rows_p, rows_p), rows_p)
+        total = mine[own, :].astype(F32)
+        for step in range(1, n_y):
+            total = total + y_in[ahead, step].astype(F32)
+        part[ahead] = total.astype(BF16)
+        for step in plane_steps(ahead):
+            xz_copy(ahead, step).start()
+
+    for h in range(2):
+        conv_inner(g_wide, backward, conv_t, h)
+
+    def branch_body(n, _):
+        branch = jnp.dot(w_out_t[...], act[:, pl.ds(al(n * 256, 256), 256)], preferred_element_type=F32)
+        for k, r in enumerate((3 - n, 4 + n)):
+            ocean = mask_ref[pl.ds(r, 1), :].astype(F32)
+            flat[pl.ds(r, C, stride=8), :] = ocean * branch[:, k * COLS : (k + 1) * COLS]
+        return 0
+
+    lax.fori_loop(0, ROWS // 2, branch_body, 0)
 
     first_k.wait()
     gk_mine[0] = (gk[core] + gk_pair[...]).astype(BF16)
@@ -549,55 +575,33 @@
     unpack_rim(place, g_rt, g_wide)
     conv_rim(g_wide, backward, conv_t)
 
-    each(n_xz, xz_copy, wait)
-    total = part[pl.ds(al(place.xz * rows_xz, rows_xz), rows_xz), :].astype(F32)
-    for step in range(1, n_xz):
-        total = total + xz_in[step].astype(F32)
-    done[place.yi, place.xz] = total.astype(BF16)
-
-    def xzg_copy(step):
-        _, device = place.xz_peer(step)
-        own = done.at[place.yi, place.xz]
-        return remote(own, own, xzg_sems, step, device)
-
-    each(n_xz, xzg_copy, start)
+    for ahead in near:
+        for step in plane_steps(ahead):
+            xz_copy(ahead, step).wait()
+    total = part[0, pl.ds(al(place.xi * rows_x, rows_x), rows_x), :].astype(F32)
+    for ahead in near:
+        for step in plane_steps(ahead):
+            total = total + xz_in[ahead, step].astype(F32)
+    done[place.yi, place.zi, place.xi] = total.astype(BF16)
+
+    def xzg_copy(ahead, step):
+        _, device = place.xz_peer(ahead, step)
+        own = done.at[place.yi, place.zi, place.xi]
+        return remote(own, own, xzg_sems, ahead * 4 + step, device)
+
+    for ahead in far:
+        for step in plane_steps(ahead):
+            xzg_copy(ahead, step).start()
     gk_finish()
     gk_finish = gk_round(1, 4, place.x_peer, gk_x, gk_x_sems)
 
     for k in range(3):
         row_wait(place, k, g_halo, g_recv)
         unpack_row(place, k, g_halo, g_wide)
-
-    def xzg_wait(step, _):
-        sender = lax.rem(place.xz + n_xz - step, n_xz)
-        wait_bytes(done.at[place.yi, sender], xzg_sems.at[1, step])
-        return 0
-
-    lax.fori_loop(1, n_xz, xzg_wait, 0)
-
-    def yg_copy(step):
-        _, device = place.y_peer(step)
-        own = done.at[place.yi]
-        return remote(own, own, yg_sems, step, device)
-
-    def across(step, index):
-        return remote(done.at[index], sums.at[index], last_sems, step, place.core_id)
-
-    each(n_y, yg_copy, start)
-    across(0, place.yi).start()
-
-    gk_finish()
-    gk_finish = gk_round(2, n_z, place.z_peer, gk_z, gk_z_sems)
-
     conv_halo(g_wide, backward, conv_t, HALO_ROWS)
     for r in range(ROWS):
         at = slice(r * COLS, (r + 1) * COLS)
         flat2[pl.ds(r, C, stride=8), :] = jnp.concatenate([conv_t[0, at, :].T, conv_t[1, at, :].T], axis=0)
-
-    gk_finish()
-    gk_all[core] = gk_mine[3]
-    last_k = remote(gk_all.at[core], gk_all.at[core], gk_last_sems, 0, place.core_id)
-    last_k.start()
 
     def out_body(group, _):
         at = pl.ds(group * 32, 32)
@@ -610,30 +614,57 @@
 
     lax.fori_loop(0, C // 32, out_body, 0)
 
-    def yg_wait(step, _):
-        sender = lax.rem(place.yi + n_y - step, n_y)
-        wait_bytes(done.at[sender], yg_sems.at[1, step])
-        across(step, sender).start()
-        return 0
-
-    lax.fori_loop(1, n_y, yg_wait, 0)
+    gk_finish()
+    gk_finish = gk_round(2, n_z, place.z_peer, gk_z, gk_z_sems)
+
+    def behind(ahead):
+        return lax.rem(place.zi + n_z - ahead, n_z)
+
+    def yg_copy(ahead, step):
+        _, device = place.y_peer(step)
+        own = done.at[place.yi, behind(ahead)]
+        return remote(own, own, yg_sems, ahead * n_y + step, device)
+
+    def across(ahead, step, y):
+        whole = done.at[y, behind(ahead)], sums.at[y, behind(ahead)]
+        return remote(*whole, last_sems, ahead * n_y + step, place.core_id)
+
+    for ahead in near:
+        for step in plane_steps(ahead):
+            x = lax.rem(place.xi + 4 - step, 4)
+            wait_bytes(done.at[place.yi, behind(ahead), x], xzg_sems.at[1, ahead * 4 + step])
+        for step in range(1, n_y):
+            yg_copy(ahead, step).start()
+        across(ahead, 0, place.yi).start()
+
+    for ahead in near:
+        for step in range(1, n_y):
+            y = lax.rem(place.yi + n_y - step, n_y)
+            wait_bytes(done.at[y, behind(ahead)], yg_sems.at[1, ahead * n_y + step])
+            across(ahead, step, y).start()
+
+    gk_finish()
+    gk_all[core] = gk_mine[3]
+    last_k = remote(gk_all.at[core], gk_all.at[core], gk_last_sems, 0, place.core_id)
+    last_k.start()
 
     wait_bytes(gk_all.at[core], gk_last_sems.at[0, 0])
     wait_bytes(gk_all.at[other], gk_last_sems.at[1, 0])
     gk_out[...] = gk_all[...]
     sums_ref[core] = done[...]
 
-    def last_wait(step, _):
-        sender = lax.rem(place.yi + n_y - step, n_y)
-        wait_bytes(done.at[sender], last_sems.at[0, step])
-        wait_bytes(sums.at[sender], last_sems.at[1, step])
-        return 0
-
-    lax.fori_loop(0, n_y, last_wait, 0)
+    for ahead in near:
+        for step in range(n_y):
+            y = lax.rem(place.yi + n_y - step, n_y)
+            wait_bytes(done.at[y, behind(ahead)], last_sems.at[0, ahead * n_y + step])
+            wait_bytes(sums.at[y, behind(ahead)], last_sems.at[1, ahead * n_y + step])
     sums_ref[other] = sums[...]
 
-    each(n_xz, xzg_copy, sent)
-    each(n_y, yg_copy, sent)
+    for ahead in near:
+        for step in plane_steps(ahead):
+            xzg_copy(ahead, step).wait_send()
+        for step in range(1, n_y):
+            yg_copy(ahead, step).wait_send()
     halo_sent(place, copies)
     halo_sent(place, g_copies)
 
@@ -663,13 +694,13 @@
 
 
 def per_device(n_lon, n_lat, ocean_state, land_mask, kernel, w_in, w_out, cotangent):
-    n_y, n_z, n_xz = n_lat // 2, n_lon // 4, n_lon
-    rows_y, rows_xz = HALF // n_y, HALF // n_y // n_xz
+    n_y, n_z = n_lat // 2, n_lon // 4
+    rows_p = HALF // n_y // n_z
     wide = pltpu.VMEM((2, 14, 144, COLS), F32)
     turned_rows = pltpu.VMEM((ROWS, COLS, C), BF16)
     table = pltpu.VMEM((2, 49, 8, COLS), F32)
     sems = lambda n: pltpu.SemaphoreType.DMA((2, n))
-    summed = pltpu.VMEM((n_y, n_xz, rows_xz, COLS), BF16)
+    summed = pltpu.VMEM((n_y, n_z, 4, rows_p // 4, COLS), BF16)
     flat = pltpu.VMEM((C * ROWS, COLS), F32)
     field = jax.ShapeDtypeStruct((C, ROWS, COLS), BF16)
     stepped, state, sums, gk = pl.pallas_call(
@@ -677,7 +708,7 @@
         out_shape=(
             field,
             field,
-            jax.ShapeDtypeStruct((2, n_y, n_xz, rows_xz, COLS), BF16),
+            jax.ShapeDtypeStruct((2, n_y, n_z, 4, rows_p // 4, COLS), BF16),
             jax.ShapeDtypeStruct((2, 64, COLS), BF16),
         ),
         in_specs=[VSPEC] * 6,
@@ -704,9 +735,9 @@
             pltpu.VMEM((2 * HALF, COLS), BF16),
             pltpu.VMEM((HALF, COLS), BF16),
             pltpu.VMEM((HALF, COLS), BF16),
-            pltpu.VMEM((n_y, rows_y, COLS), BF16),
-            pltpu.VMEM((rows_y, COLS), BF16),
-            pltpu.VMEM((n_xz, rows_xz, COLS), BF16),
+            pltpu.VMEM((n_z, n_y, rows_p, COLS), BF16),
+            pltpu.VMEM((n_z, rows_p, COLS), BF16),
+            pltpu.VMEM((n_z, 4, rows_p // 4, COLS), BF16),
             summed,
             summed,
             pltpu.VMEM((2, 8, 8, COLS), F32),
@@ -718,11 +749,11 @@
             pltpu.VMEM((n_z, 64, COLS), BF16),
             pltpu.VMEM((2, 64, COLS), BF16),
             sems(1),
-            sems(n_y),
-            sems(n_xz),
-            sems(n_xz),
-            sems(n_y),
-            sems(n_y),
+            sems(n_z * n_y),
+            sems(n_z * 4),
+            sems(n_z * 4),
+            sems(n_z * n_y),
+            sems(n_z * n_y),
             sems(1),
             sems(n_y),
             sems(4),

time: 76 us -> 76.1 us (level)
  no operation moved by 1% of the time
where the time goes in v4:
time: 76.1 us; the launch traced here: 75.9 us
  Pallas kernels  75.3 us (99%)
    pallas_call x1, Pallas kernels, per_device(): pl.pallas_call(functools.partial(whole_kernel, n_lon, n_lat), out_shape=(...  72 us
    pallas_call x1, Pallas kernels, per_device(): pl.pallas_call(finish_kernel, out_shape=(field, field, jax.ShapeDtypeStru...  3.25 us

profile of v4, /device:TPU:1, one launch (start us, length us, event | category | flops | bytes accessed | tf_op | source)
XLA Modules:
  0.0 75.9 jit_solution(15381611406699706473)
XLA Ops:
  0.6 72.0 %convnext.1 = (bf16[256,8,128]{2,1,0:T(8,128)(2,1)}, bf16[256,8,128]{2,1,0:T(8,128)(2,1)}, bf16[2,4,8,4,16,128]{5,4,3,2,1,0:T(8,128)(2,1)}, bf16[2,64,128]{2,1,0:T(8,128)(2,1)}) custom-call(bf16[256,8,128]{2,1,0:T(8,128)(2,1)} %x_ref.1, s32[8,128]{1,0:T(8,128)} %mask_ref.1, bf16[49,256]{1,0:T(8,128)(2,1)} %taps_ref.1, bf16[256,1024]{1,0:T(8,128)(2,1)} %w_in_ref.1, ...), custom_call_target="tpu_custom_call" | custom-call | tf_op jit(solution)/shard_map/convnext/pallas_call | solution.py:706
  72.7 3.2 %finish.1 = (bf16[256,8,128]{2,1,0:T(8,128)(2,1)}, bf16[256,8,128]{2,1,0:T(8,128)(2,1)}, f32[49,256]{1,0:T(8,128)}, f32[256,1024]{1,0:T(8,128)}, f32[1024,256]{1,0:T(8,128)}) custom-call(bf16[256,8,128]{2,1,0:T(8,128)(2,1)} %get-tuple-element.9.stepped_in, bf16[256,8,128]{2,1,0:T(8,128)(2,1)} %get-tuple-element.10.state_in, bf16[2,2048,128]{2,1,0:T(8,128)(2,1)} %bitcast.1, ...), custom_call_target="tpu_custom_call" | custom-call | tf_op jit(solution)/shard_map/finish/pallas_call | solution.py:768

commit v5 on v4

--- a/solution.py
+++ b/solution.py
@@ -371,6 +371,14 @@
     for i in range(ROWS):
         lay_row(i, flat[pl.ds(i, C, stride=8), :].astype(BF16), ident, wide, rows_t, edge_f)
     lay_edges(edge_f, edges)
+    w_in_t[...] = w_in_ref[...].astype(F32).T.astype(BF16)
+    w_out_t[...] = w_out_ref[...].astype(F32).T.astype(BF16)
+    pl.semaphore_wait(barrier, count + n_y + 4 * n_z - 1)
+    copies = halo_copies(place, rows_t, edges, halo, rt, send_sem, recv_sem)
+    halo_start(place, copies, edges, rt, recv_sem)
+    for k in range(3):
+        row_start(place, copies, k)
+
     crown = place.crown == 1
     table = taps_ref[...].astype(F32)
     for t in range(49):
@@ -386,24 +394,16 @@
     def backward(h, a, q, r):
         return taps_n[h, 7 * a + q] if r >= 11 else taps[h, 48 - 7 * a - q]
 
-    conv_inner(wide, forward, conv_t, 0)
-    w_in_t[...] = w_in_ref[...].astype(F32).T.astype(BF16)
-    w_out_t[...] = w_out_ref[...].astype(F32).T.astype(BF16)
+    for h in range(2):
+        conv_inner(wide, forward, conv_t, h)
     flat[...] = cot_ref[...].astype(F32).reshape(C * ROWS, COLS)
     for r in range(ROWS):
         ocean = mask_ref[pl.ds(r, 1), :].astype(F32)
         gb[:, PLACE[r] * COLS : (PLACE[r] + 1) * COLS] = (ocean * flat[pl.ds(r, C, stride=8), :]).astype(BF16)
 
-    pl.semaphore_wait(barrier, count + n_y + 4 * n_z - 1)
-    copies = halo_copies(place, rows_t, edges, halo, rt, send_sem, recv_sem)
-    halo_start(place, copies, edges, rt, recv_sem)
-    row_start(place, copies, 0)
-    conv_inner(wide, forward, conv_t, 1)
-    row_start(place, copies, 1)
     rim_wait(place, rt, recv_sem)
     unpack_rim(place, rt, wide)
     conv_rim(wide, forward, conv_t)
-    row_start(place, copies, 2)
 
     def cells_body(n, _):
         for k in range(3):
@@ -493,9 +493,6 @@
         lay_row(r, g_conv.astype(BF16), ident, g_wide, g_rows, edge_f)
     lay_edges(edge_f, g_edges)
     g_copies = halo_copies(place, g_rows, g_edges, g_halo, g_rt, g_send, g_recv)
-    halo_start(place, g_copies, g_edges, g_rt, g_recv)
-    for k in range(3):
-        row_start(place, g_copies, k)
 
     first.wait()
 
@@ -540,6 +537,9 @@
         part[ahead] = total.astype(BF16)
         for step in plane_steps(ahead):
             xz_copy(ahead, step).start()
+    halo_start(place, g_copies, g_edges, g_rt, g_recv)
+    for k in range(3):
+        row_start(place, g_copies, k)
 
     for h in range(2):
         conv_inner(g_wide, backward, conv_t, h)
@@ -571,9 +571,6 @@
         return finish
 
     gk_finish = gk_round(0, n_y, lambda step: place.y_peer(step)[1], gk_y, gk_y_sems)
-    rim_wait(place, g_rt, g_recv)
-    unpack_rim(place, g_rt, g_wide)
-    conv_rim(g_wide, backward, conv_t)
 
     for ahead in near:
         for step in plane_steps(ahead):
@@ -595,6 +592,32 @@
     gk_finish()
     gk_finish = gk_round(1, 4, place.x_peer, gk_x, gk_x_sems)
 
+    rim_wait(place, g_rt, g_recv)
+    unpack_rim(place, g_rt, g_wide)
+    conv_rim(g_wide, backward, conv_t)
+
+    def behind(ahead):
+        return lax.rem(place.zi + n_z - ahead, n_z)
+
+    def yg_copy(ahead, step):
+        _, device = place.y_peer(step)
+        own = done.at[place.yi, behind(ahead)]
+        return remote(own, own, yg_sems, ahead * n_y + step, device)
+
+    def across(ahead, step, y):
+        whole = done.at[y, behind(ahead)], sums.at[y, behind(ahead)]
+        return remote(*whole, last_sems, ahead * n_y + step, place.core_id)
+
+    for ahead in near:
+        for step in plane_steps(ahead):
+            x = lax.rem(place.xi + 4 - step, 4)
+            wait_bytes(done.at[place.yi, behind(ahead), x], xzg_sems.at[1, ahead * 4 + step])
+        for step in range(1, n_y):
+            yg_copy(ahead, step).start()
+        across(ahead, 0, place.yi).start()
+
+    gk_finish()
+    gk_finish = gk_round(2, n_z, place.z_peer, gk_z, gk_z_sems)
     for k in range(3):
         row_wait(place, k, g_halo, g_recv)
         unpack_row(place, k, g_halo, g_wide)
@@ -613,29 +636,6 @@
         return 0
 
     lax.fori_loop(0, C // 32, out_body, 0)
-
-    gk_finish()
-    gk_finish = gk_round(2, n_z, place.z_peer, gk_z, gk_z_sems)
-
-    def behind(ahead):
-        return lax.rem(place.zi + n_z - ahead, n_z)
-
-    def yg_copy(ahead, step):
-        _, device = place.y_peer(step)
-        own = done.at[place.yi, behind(ahead)]
-        return remote(own, own, yg_sems, ahead * n_y + step, device)
-
-    def across(ahead, step, y):
-        whole = done.at[y, behind(ahead)], sums.at[y, behind(ahead)]
-        return remote(*whole, last_sems, ahead * n_y + step, place.core_id)
-
-    for ahead in near:
-        for step in plane_steps(ahead):
-            x = lax.rem(place.xi + 4 - step, 4)
-            wait_bytes(done.at[place.yi, behind(ahead), x], xzg_sems.at[1, ahead * 4 + step])
-        for step in range(1, n_y):
-            yg_copy(ahead, step).start()
-        across(ahead, 0, place.yi).start()
 
     for ahead in near:
         for step in range(1, n_y):

time: 76.1 us -> 75.6 us (level)
  no operation moved by 1% of the time
where the time goes in v5:
time: 75.6 us; the launch traced here: 75.5 us
  Pallas kernels  74.9 us (99%)
    pallas_call x1, Pallas kernels, per_device(): pl.pallas_call(functools.partial(whole_kernel, n_lon, n_lat), out_shape=(...  71.6 us
    pallas_call x1, Pallas kernels, per_device(): pl.pallas_call(finish_kernel, out_shape=(field, field, jax.ShapeDtypeStru...  3.25 us

profile of v5, /device:TPU:1, one launch (start us, length us, event | category | flops | bytes accessed | tf_op | source)
XLA Modules:
  0.0 75.5 jit_solution(10813892399140495171)
XLA Ops:
  0.6 71.6 %convnext.1 = (bf16[256,8,128]{2,1,0:T(8,128)(2,1)}, bf16[256,8,128]{2,1,0:T(8,128)(2,1)}, bf16[2,4,8,4,16,128]{5,4,3,2,1,0:T(8,128)(2,1)}, bf16[2,64,128]{2,1,0:T(8,128)(2,1)}) custom-call(bf16[256,8,128]{2,1,0:T(8,128)(2,1)} %x_ref.1, s32[8,128]{1,0:T(8,128)} %mask_ref.1, bf16[49,256]{1,0:T(8,128)(2,1)} %taps_ref.1, bf16[256,1024]{1,0:T(8,128)(2,1)} %w_in_ref.1, ...), custom_call_target="tpu_custom_call" | custom-call | tf_op jit(solution)/shard_map/convnext/pallas_call | solution.py:706
  72.3 3.2 %finish.1 = (bf16[256,8,128]{2,1,0:T(8,128)(2,1)}, bf16[256,8,128]{2,1,0:T(8,128)(2,1)}, f32[49,256]{1,0:T(8,128)}, f32[256,1024]{1,0:T(8,128)}, f32[1024,256]{1,0:T(8,128)}) custom-call(bf16[256,8,128]{2,1,0:T(8,128)(2,1)} %get-tuple-element.9.stepped_in, bf16[256,8,128]{2,1,0:T(8,128)(2,1)} %get-tuple-element.10.state_in, bf16[2,2048,128]{2,1,0:T(8,128)(2,1)} %bitcast.1, ...), custom_call_target="tpu_custom_call" | custom-call | tf_op jit(solution)/shard_map/finish/pallas_call | solution.py:768

commit v6 on v5

--- a/solution.py
+++ b/solution.py
@@ -352,19 +352,18 @@
     core, other = place.core, 1 - place.core
 
     barrier = pltpu.get_barrier_semaphore()
+    def greet_y(step, _):
+        signal(barrier, place.y_peer(step)[1])
+        return 0
+
+    def greet_xz(n, _):
+        signal(barrier, place.xz_peer(n // 4, lax.rem(n, 4))[1])
+        return 0
+
+    lax.fori_loop(1, 4 * n_z, greet_xz, 0)
+    lax.fori_loop(1, n_y, greet_y, 0)
     count = greet_halo(place, barrier)
     signal(barrier, place.core_id)
-
-    def greet_y(step, _):
-        signal(barrier, place.y_peer(step)[1])
-        return 0
-
-    def greet_xz(n, _):
-        signal(barrier, place.xz_peer(n // 4, lax.rem(n, 4))[1])
-        return 0
-
-    lax.fori_loop(1, n_y, greet_y, 0)
-    lax.fori_loop(1, 4 * n_z, greet_xz, 0)
 
     ident = square(COLS, lambda s, t: s == t)
     flat[...] = x_ref[...].astype(F32).reshape(C * ROWS, COLS)
@@ -376,8 +375,7 @@
     pl.semaphore_wait(barrier, count + n_y + 4 * n_z - 1)
     copies = halo_copies(place, rows_t, edges, halo, rt, send_sem, recv_sem)
     halo_start(place, copies, edges, rt, recv_sem)
-    for k in range(3):
-        row_start(place, copies, k)
+    row_start(place, copies, 0)
 
     crown = place.crown == 1
     table = taps_ref[...].astype(F32)
@@ -396,6 +394,7 @@
 
     for h in range(2):
         conv_inner(wide, forward, conv_t, h)
+        row_start(place, copies, 1 + h)
     flat[...] = cot_ref[...].astype(F32).reshape(C * ROWS, COLS)
     for r in range(ROWS):
         ocean = mask_ref[pl.ds(r, 1), :].astype(F32)

time: 75.6 us -> 74.6 us (0.987)
  Pallas kernels: 74.9 us -> 73.9 us
    pallas_call x1, Pallas kernels: 71.6 us -> 70.6 us  [per_device(): pl.pallas_call(functools.partial(whole_kernel, n_lon, n_lat), out_shape=(...]
where the time goes in v6:
time: 74.6 us; the launch traced here: 74.5 us
  Pallas kernels  73.9 us (99%)
    pallas_call x1, Pallas kernels, per_device(): pl.pallas_call(functools.partial(whole_kernel, n_lon, n_lat), out_shape=(...  70.6 us
    pallas_call x1, Pallas kernels, per_device(): pl.pallas_call(finish_kernel, out_shape=(field, field, jax.ShapeDtypeStru...  3.25 us

profile of v6, /device:TPU:1, one launch (start us, length us, event | category | flops | bytes accessed | tf_op | source)
XLA Modules:
  0.0 74.5 jit_solution(7673270360178206983)
XLA Ops:
  0.6 70.6 %convnext.1 = (bf16[256,8,128]{2,1,0:T(8,128)(2,1)}, bf16[256,8,128]{2,1,0:T(8,128)(2,1)}, bf16[2,4,8,4,16,128]{5,4,3,2,1,0:T(8,128)(2,1)}, bf16[2,64,128]{2,1,0:T(8,128)(2,1)}) custom-call(bf16[256,8,128]{2,1,0:T(8,128)(2,1)} %x_ref.1, s32[8,128]{1,0:T(8,128)} %mask_ref.1, bf16[49,256]{1,0:T(8,128)(2,1)} %taps_ref.1, bf16[256,1024]{1,0:T(8,128)(2,1)} %w_in_ref.1, ...), custom_call_target="tpu_custom_call" | custom-call | tf_op jit(solution)/shard_map/convnext/pallas_call | solution.py:705
  71.3 3.2 %finish.1 = (bf16[256,8,128]{2,1,0:T(8,128)(2,1)}, bf16[256,8,128]{2,1,0:T(8,128)(2,1)}, f32[49,256]{1,0:T(8,128)}, f32[256,1024]{1,0:T(8,128)}, f32[1024,256]{1,0:T(8,128)}) custom-call(bf16[256,8,128]{2,1,0:T(8,128)(2,1)} %get-tuple-element.9.stepped_in, bf16[256,8,128]{2,1,0:T(8,128)(2,1)} %get-tuple-element.10.state_in, bf16[2,2048,128]{2,1,0:T(8,128)(2,1)} %bitcast.1, ...), custom_call_target="tpu_custom_call" | custom-call | tf_op jit(solution)/shard_map/finish/pallas_call | solution.py:767

commit v7 on v6

--- a/solution.py
+++ b/solution.py
@@ -261,7 +261,6 @@
 
 
 LOCAL_ROWS = tuple(range(3, 11))
-HALO_ROWS = (0, 1, 2, 11, 12, 13)
 PLACE = (6, 4, 2, 0, 1, 3, 5, 7)
 
 
@@ -521,6 +520,10 @@
     first_k = remote(gk.at[other], gk_pair, gk_core, 0, place.core_id)
     first_k.start()
 
+    halo_start(place, g_copies, g_edges, g_rt, g_recv)
+    for k in range(3):
+        row_start(place, g_copies, k)
+
     def xz_copy(ahead, step):
         x, device = place.xz_peer(ahead, step)
         src = part.at[ahead, pl.ds(al(x * rows_x, rows_x), rows_x)]
@@ -536,21 +539,8 @@
         part[ahead] = total.astype(BF16)
         for step in plane_steps(ahead):
             xz_copy(ahead, step).start()
-    halo_start(place, g_copies, g_edges, g_rt, g_recv)
-    for k in range(3):
-        row_start(place, g_copies, k)
-
-    for h in range(2):
-        conv_inner(g_wide, backward, conv_t, h)
-
-    def branch_body(n, _):
-        branch = jnp.dot(w_out_t[...], act[:, pl.ds(al(n * 256, 256), 256)], preferred_element_type=F32)
-        for k, r in enumerate((3 - n, 4 + n)):
-            ocean = mask_ref[pl.ds(r, 1), :].astype(F32)
-            flat[pl.ds(r, C, stride=8), :] = ocean * branch[:, k * COLS : (k + 1) * COLS]
-        return 0
-
-    lax.fori_loop(0, ROWS // 2, branch_body, 0)
+
+    conv_inner(g_wide, backward, conv_t, 0)
 
     first_k.wait()
     gk_mine[0] = (gk[core] + gk_pair[...]).astype(BF16)
@@ -591,9 +581,36 @@
     gk_finish()
     gk_finish = gk_round(1, 4, place.x_peer, gk_x, gk_x_sems)
 
+    conv_inner(g_wide, backward, conv_t, 1)
+
+    def branch_body(n, _):
+        branch = jnp.dot(w_out_t[...], act[:, pl.ds(al(n * 256, 256), 256)], preferred_element_type=F32)
+        for k, r in enumerate((3 - n, 4 + n)):
+            ocean = mask_ref[pl.ds(r, 1), :].astype(F32)
+            flat[pl.ds(r, C, stride=8), :] = ocean * branch[:, k * COLS : (k + 1) * COLS]
+        return 0
+
+    lax.fori_loop(0, ROWS // 2, branch_body, 0)
+
+    def stepped_body(group, _):
+        at = pl.ds(group * 32, 32)
+        moved = flat[pl.ds(al(group * 256, 256), 256), :].reshape(32, ROWS, COLS)
+        stepped_ref[at] = (x_ref[at].astype(F32) + moved).astype(BF16)
+        return 0
+
+    lax.fori_loop(0, C // 32, stepped_body, 0)
+
     rim_wait(place, g_rt, g_recv)
     unpack_rim(place, g_rt, g_wide)
     conv_rim(g_wide, backward, conv_t)
+
+    def halo_row(k):
+        row_wait(place, k, g_halo, g_recv)
+        unpack_row(place, k, g_halo, g_wide)
+        conv_halo(g_wide, backward, conv_t, (2 - k, 11 + k))
+
+    halo_row(0)
+    halo_row(1)
 
     def behind(ahead):
         return lax.rem(place.zi + n_z - ahead, n_z)
@@ -617,24 +634,19 @@
 
     gk_finish()
     gk_finish = gk_round(2, n_z, place.z_peer, gk_z, gk_z_sems)
-    for k in range(3):
-        row_wait(place, k, g_halo, g_recv)
-        unpack_row(place, k, g_halo, g_wide)
-    conv_halo(g_wide, backward, conv_t, HALO_ROWS)
+    halo_row(2)
     for r in range(ROWS):
         at = slice(r * COLS, (r + 1) * COLS)
         flat2[pl.ds(r, C, stride=8), :] = jnp.concatenate([conv_t[0, at, :].T, conv_t[1, at, :].T], axis=0)
 
-    def out_body(group, _):
+    def state_body(group, _):
         at = pl.ds(group * 32, 32)
         rows_at = pl.ds(al(group * 256, 256), 256)
-        moved = flat[rows_at, :].reshape(32, ROWS, COLS)
-        stepped_ref[at] = (x_ref[at].astype(F32) + moved).astype(BF16)
         moved = flat2[rows_at, :].reshape(32, ROWS, COLS)
         state_ref[at] = (cot_ref[at].astype(F32) + moved).astype(BF16)
         return 0
 
-    lax.fori_loop(0, C // 32, out_body, 0)
+    lax.fori_loop(0, C // 32, state_body, 0)
 
     for ahead in near:
         for step in range(1, n_y):

time: 74.6 us -> 76.4 us (1.024)
  Pallas kernels: 73.9 us -> 75.6 us
    pallas_call x1, Pallas kernels: 70.6 us -> 72.4 us  [per_device(): pl.pallas_call(functools.partial(whole_kernel, n_lon, n_lat), out_shape=(...]
where the time goes in v7:
time: 76.4 us; the launch traced here: 76.3 us
  Pallas kernels  75.6 us (99%)
    pallas_call x1, Pallas kernels, per_device(): pl.pallas_call(functools.partial(whole_kernel, n_lon, n_lat), out_shape=(...  72.4 us
    pallas_call x1, Pallas kernels, per_device(): pl.pallas_call(finish_kernel, out_shape=(field, field, jax.ShapeDtypeStru...  3.25 us

profile of v7, /device:TPU:1, one launch (start us, length us, event | category | flops | bytes accessed | tf_op | source)
XLA Modules:
  0.0 76.3 jit_solution(1877739753665704347)
XLA Ops:
  0.6 72.4 %convnext.1 = (bf16[256,8,128]{2,1,0:T(8,128)(2,1)}, bf16[256,8,128]{2,1,0:T(8,128)(2,1)}, bf16[2,4,8,4,16,128]{5,4,3,2,1,0:T(8,128)(2,1)}, bf16[2,64,128]{2,1,0:T(8,128)(2,1)}) custom-call(bf16[256,8,128]{2,1,0:T(8,128)(2,1)} %x_ref.1, s32[8,128]{1,0:T(8,128)} %mask_ref.1, bf16[49,256]{1,0:T(8,128)(2,1)} %taps_ref.1, bf16[256,1024]{1,0:T(8,128)(2,1)} %w_in_ref.1, ...), custom_call_target="tpu_custom_call" | custom-call | tf_op jit(solution)/shard_map/convnext/pallas_call | solution.py:717
  73.0 3.2 %finish.1 = (bf16[256,8,128]{2,1,0:T(8,128)(2,1)}, bf16[256,8,128]{2,1,0:T(8,128)(2,1)}, f32[49,256]{1,0:T(8,128)}, f32[256,1024]{1,0:T(8,128)}, f32[1024,256]{1,0:T(8,128)}) custom-call(bf16[256,8,128]{2,1,0:T(8,128)(2,1)} %get-tuple-element.9.stepped_in, bf16[256,8,128]{2,1,0:T(8,128)(2,1)} %get-tuple-element.10.state_in, bf16[2,2048,128]{2,1,0:T(8,128)(2,1)} %bitcast.1, ...), custom_call_target="tpu_custom_call" | custom-call | tf_op jit(solution)/shard_map/finish/pallas_call | solution.py:779

commit v8 on v6

--- a/solution.py
+++ b/solution.py
@@ -515,6 +515,10 @@
         for step in range(1, n_y):
             y_copy(ahead, step).start()
 
+    halo_start(place, g_copies, g_edges, g_rt, g_recv)
+    for k in range(3):
+        row_start(place, g_copies, k)
+
     tap_sums(wide, g_wide, tap_acc)
     for h in range(2):
         gk[h] = tap_acc[h].reshape(64, COLS)
@@ -536,21 +540,8 @@
         part[ahead] = total.astype(BF16)
         for step in plane_steps(ahead):
             xz_copy(ahead, step).start()
-    halo_start(place, g_copies, g_edges, g_rt, g_recv)
-    for k in range(3):
-        row_start(place, g_copies, k)
-
-    for h in range(2):
-        conv_inner(g_wide, backward, conv_t, h)
-
-    def branch_body(n, _):
-        branch = jnp.dot(w_out_t[...], act[:, pl.ds(al(n * 256, 256), 256)], preferred_element_type=F32)
-        for k, r in enumerate((3 - n, 4 + n)):
-            ocean = mask_ref[pl.ds(r, 1), :].astype(F32)
-            flat[pl.ds(r, C, stride=8), :] = ocean * branch[:, k * COLS : (k + 1) * COLS]
-        return 0
-
-    lax.fori_loop(0, ROWS // 2, branch_body, 0)
+
+    conv_inner(g_wide, backward, conv_t, 0)
 
     first_k.wait()
     gk_mine[0] = (gk[core] + gk_pair[...]).astype(BF16)
@@ -590,6 +581,17 @@
             xzg_copy(ahead, step).start()
     gk_finish()
     gk_finish = gk_round(1, 4, place.x_peer, gk_x, gk_x_sems)
+
+    conv_inner(g_wide, backward, conv_t, 1)
+
+    def branch_body(n, _):
+        branch = jnp.dot(w_out_t[...], act[:, pl.ds(al(n * 256, 256), 256)], preferred_element_type=F32)
+        for k, r in enumerate((3 - n, 4 + n)):
+            ocean = mask_ref[pl.ds(r, 1), :].astype(F32)
+            flat[pl.ds(r, C, stride=8), :] = ocean * branch[:, k * COLS : (k + 1) * COLS]
+        return 0
+
+    lax.fori_loop(0, ROWS // 2, branch_body, 0)
 
     rim_wait(place, g_rt, g_recv)
     unpack_rim(place, g_rt, g_wide)

time: 74.6 us -> 73.8 us (0.989)
  Pallas kernels: 73.9 us -> 73 us
    pallas_call x1, Pallas kernels: 70.6 us -> 69.8 us  [per_device(): pl.pallas_call(functools.partial(whole_kernel, n_lon, n_lat), out_shape=(...]
where the time goes in v8:
time: 73.8 us; the launch traced here: 73.7 us
  Pallas kernels  73 us (99%)
    pallas_call x1, Pallas kernels, per_device(): pl.pallas_call(functools.partial(whole_kernel, n_lon, n_lat), out_shape=(...  69.8 us
    pallas_call x1, Pallas kernels, per_device(): pl.pallas_call(finish_kernel, out_shape=(field, field, jax.ShapeDtypeStru...  3.25 us

profile of v8, /device:TPU:1, one launch (start us, length us, event | category | flops | bytes accessed | tf_op | source)
XLA Modules:
  0.0 73.7 jit_solution(7792929636938292885)
XLA Ops:
  0.6 69.8 %convnext.1 = (bf16[256,8,128]{2,1,0:T(8,128)(2,1)}, bf16[256,8,128]{2,1,0:T(8,128)(2,1)}, bf16[2,4,8,4,16,128]{5,4,3,2,1,0:T(8,128)(2,1)}, bf16[2,64,128]{2,1,0:T(8,128)(2,1)}) custom-call(bf16[256,8,128]{2,1,0:T(8,128)(2,1)} %x_ref.1, s32[8,128]{1,0:T(8,128)} %mask_ref.1, bf16[49,256]{1,0:T(8,128)(2,1)} %taps_ref.1, bf16[256,1024]{1,0:T(8,128)(2,1)} %w_in_ref.1, ...), custom_call_target="tpu_custom_call" | custom-call | tf_op jit(solution)/shard_map/convnext/pallas_call | solution.py:707
  70.4 3.2 %finish.1 = (bf16[256,8,128]{2,1,0:T(8,128)(2,1)}, bf16[256,8,128]{2,1,0:T(8,128)(2,1)}, f32[49,256]{1,0:T(8,128)}, f32[256,1024]{1,0:T(8,128)}, f32[1024,256]{1,0:T(8,128)}) custom-call(bf16[256,8,128]{2,1,0:T(8,128)(2,1)} %get-tuple-element.9.stepped_in, bf16[256,8,128]{2,1,0:T(8,128)(2,1)} %get-tuple-element.10.state_in, bf16[2,2048,128]{2,1,0:T(8,128)(2,1)} %bitcast.1, ...), custom_call_target="tpu_custom_call" | custom-call | tf_op jit(solution)/shard_map/finish/pallas_call | solution.py:769
